TPU v7x, 128 devices: a whole 4x4x4 slice. The times are simulated.
128 devices in a mesh: dp: 32 (over y_lo, x, z), mp: 4 (over y_hi, core).
Axes of the slice: x: 4, y: 4 (y_hi: 2, y_lo: 2; y = y_hi * 2 + y_lo), z: 4, core: 2. Of those that a mesh axis runs over, the one named last changes fastest.
Arguments:
- stream: bfloat16 [32, 512, 2048], P('dp'), may hold values from -6 to 6
- code_ids: int32 [32, 512], P('dp'), may hold values from 0 to 4095
- segment_ids: int32 [32, 512], P('dp'), may hold values from 0 to 3, never falling along the last dimension, each value on 1 to 256 neighbouring positions
- padding: int32 [32, 512], P('dp'), may hold values from 0 to 1, as said below
- codebook: bfloat16 [4096, 2048], replicated, may hold values from -6 to 6
- norm1_gain: bfloat16 [2048], P('dp'), may hold values from 0.099609375 to 1.8984375
- norm1_shift: bfloat16 [2048], P('dp'), may hold values from -3 to 3
- w_qkv: bfloat16 [2048, 3, 2048], P('dp', None, 'mp'), may hold values from -0.125 to 0.125
- w_out: bfloat16 [2048, 2048], P('dp', 'mp'), may hold values from -0.75 to 0.75
- norm2_gain: bfloat16 [2048], P('dp'), may hold values from 0.099609375 to 1.8984375
- norm2_shift: bfloat16 [2048], P('dp'), may hold values from -3 to 3
- w_up: bfloat16 [2048, 8192], P('dp', 'mp'), may hold values from -0.125 to 0.125
- w_down: bfloat16 [2048, 8192], P('dp', 'mp'), may hold values from -0.0625 to 0.0625
- cotangent: bfloat16 [32, 512, 2048], P('dp'), may hold values from -6 to 6
Outputs:
- layer_out: float32 [32, 512, 2048], P('dp')
- input_grad: float32 [32, 512, 2048], P('dp')
- grad_norm1_gain: float32 [2048], P('dp')
- grad_norm1_shift: float32 [2048], P('dp')
- grad_w_qkv: float32 [2048, 3, 2048], P('dp', None, 'mp')
- grad_w_out: float32 [2048, 2048], P('dp', 'mp')
- grad_norm2_gain: float32 [2048], P('dp')
- grad_norm2_shift: float32 [2048], P('dp')
- grad_w_up: float32 [2048, 8192], P('dp', 'mp')
- grad_w_down: float32 [2048, 8192], P('dp', 'mp')
Inputs may be any that keep to these rules, and one draw needn't show every extreme that they name: In each row the real tokens come first and the last 1 to 128 positions are padding. `segment_ids`: episode numbers never fall along a row; an episode spans at most 256 positions.
All inputs are finite; a program needn't handle non-finite values.
Results may differ from a plain program's by a relative error of at most 0.028.
Values may be sent and summed in bfloat16 or wider, within the bound.
A program may use at most 192 MiB of HBM per device.

v0:
```python
import jax
import jax.numpy as jnp
from jax import lax
from jax.sharding import PartitionSpec as P

HEAD = 128


masked_score = -1000000000.0
epsilon = 1e-05


def split_up(value, dim, peers):
    before, after = (value.shape[:dim], value.shape[dim + 1 :])
    return jnp.moveaxis(value.reshape(*before, peers, -1, *after), dim, 0)


def sent_and_summed(value, axis, dim):
    pieces = split_up(value, dim, lax.axis_size(axis))
    arrived = lax.all_to_all(pieces, axis, split_axis=0, concat_axis=0, tiled=True)
    return arrived.sum(axis=0)


def from_everyone(value, axis):
    peers = lax.axis_size(axis)
    return lax.all_to_all(
        jnp.broadcast_to(value[None], (peers, *value.shape)), axis, 0, 0, tiled=True
    )


def in_order(pieces, dim):
    lengths = list(pieces.shape[1:])
    lengths[dim] *= pieces.shape[0]
    return jnp.moveaxis(pieces, 0, dim).reshape(lengths)


def collect(value, axis, dim):
    pieces = from_everyone(value, axis)
    return in_order(pieces, dim)


def gather_turned(arrays, axis, dims):
    turned = [jnp.moveaxis(a, dim, 0) for a, dim in zip(arrays, dims)]
    both = jnp.concatenate([t.reshape(len(t), -1) for t in turned], axis=1)
    filled, at, done = (lax.all_gather(both, axis, axis=0, tiled=True), 0, [])
    for t, dim in zip(turned, dims):
        piece = filled[:, at : at + t[0].size].reshape(-1, *t.shape[1:])
        done.append(jnp.moveaxis(piece, 0, dim))
        at += t[0].size
    return tuple(done)


def in_one_piece(arrays, axis, dim, along):
    columns = [a.reshape(*a.shape[:along], -1) for a in arrays]
    both = jnp.concatenate(columns, axis=along)
    filled, at, done = (lax.psum_scatter(both, axis, scatter_dimension=dim, tiled=True), 0, [])
    for a, column in zip(arrays, columns):
        piece = filled[..., at : at + column.shape[along]]
        done.append(piece.reshape(*piece.shape[:along], *a.shape[along:]))
        at += column.shape[along]
    return tuple(done)


def in_one_piece_2(arrays, axis, dim, along):
    widths = [a.shape[along] for a in arrays]
    both = jnp.concatenate(arrays, axis=along)
    filled = lax.all_gather(both, axis, axis=dim, tiled=True)
    return tuple(jnp.split(filled, [sum(widths[:k]) for k in range(1, len(widths))], axis=along))


def over_copies(value, axis):
    everything = from_everyone(value, axis)
    return jnp.sum(everything, axis=0)


def together(arrays, axis):
    ends = [0]
    for a in arrays:
        ends.append(ends[-1] + a.size)
    running = over_copies(jnp.concatenate([a.ravel() for a in arrays]), axis)
    return tuple((running[b:e].reshape(a.shape) for a, b, e in zip(arrays, ends, ends[1:])))


def standardize(value):
    mean = jnp.mean(value, axis=-1, keepdims=True)
    centered = value - mean
    scale_inv = lax.rsqrt(jnp.mean(centered * centered, axis=-1, keepdims=True) + epsilon)
    return (centered * scale_inv, scale_inv)


def norm_back(grad_normed_out, normed, scale_inv, gain):
    scaled = grad_normed_out * gain
    mean_one = jnp.mean(scaled, axis=-1, keepdims=True)
    mean_two = jnp.mean(scaled * normed, axis=-1, keepdims=True)
    grad_value = scale_inv * (scaled - mean_one - normed * mean_two)
    grad_gain = jnp.sum(grad_normed_out * normed, axis=(0, 1))
    grad_shift = jnp.sum(grad_normed_out, axis=(0, 1))
    return (grad_value, grad_gain, grad_shift)


def visible(segment_ids, padding):
    seq_len = segment_ids.shape[1]
    position = jnp.arange(seq_len)
    causal = position[None, :] <= position[:, None]
    itself = position[None, :] == position[:, None]
    same = segment_ids[:, :, None] == segment_ids[:, None, :]
    live = (padding[:, None, :] == 1) | itself[None]
    return same & causal[None] & live


def score_block(query_heads, key_heads, allowed):
    scores = jnp.einsum(
        "rqhe,rkhe->rhqk", query_heads, key_heads, preferred_element_type=jnp.float32
    ) * HEAD ** (-0.5)
    return jnp.where(allowed[:, None], scores, masked_score)


def share_sum(value):
    return sent_and_summed(value, "mp", 1)


def gather_low(value):
    return collect(value, "mp", 1)


def on_device(
    stream,
    code_ids,
    segment_ids,
    padding,
    codebook,
    norm1_gain,
    norm1_shift,
    w_qkv,
    w_out,
    norm2_gain,
    norm2_shift,
    w_up,
    w_down,
    cotangent,
):
    row_count, seq_len, width = stream.shape
    local_width = w_qkv.shape[2]
    local_heads = local_width // HEAD
    share_len = seq_len // lax.axis_size("mp")
    share_start = lax.axis_index("mp") * share_len
    inputs = stream.astype(jnp.float32) + jnp.take(codebook, code_ids, axis=0).astype(jnp.float32)
    allowed = visible(segment_ids, padding)
    gain_one, shift_one, qkv_full, out_full = gather_turned(
        (norm1_gain, norm1_shift, w_qkv, w_out), "dp", (0, 0, 0, 0)
    )
    normed_one, inv_one = standardize(inputs)
    attn_in = (normed_one * gain_one.astype(jnp.float32) + shift_one.astype(jnp.float32)).astype(
        jnp.bfloat16
    )
    projected = jnp.einsum(
        "rsd,dtf->trsf", attn_in, qkv_full, preferred_element_type=jnp.float32
    ).astype(jnp.bfloat16)
    query_heads = projected[0].reshape(row_count, seq_len, local_heads, HEAD)
    key_heads = projected[1].reshape(row_count, seq_len, local_heads, HEAD)
    value_heads = projected[2].reshape(row_count, seq_len, local_heads, HEAD)
    scores = score_block(query_heads, key_heads, allowed)
    row_max = jnp.max(scores, axis=-1, keepdims=True)
    expd = jnp.exp(scores - row_max)
    row_sum = jnp.sum(expd, axis=-1, keepdims=True)
    log_total = row_max + jnp.log(row_sum)
    prob_low = (expd / row_sum).astype(jnp.bfloat16)
    attended = jnp.einsum(
        "rhqk,rkhe->rqhe", prob_low, value_heads, preferred_element_type=jnp.float32
    )
    attended = attended.reshape(row_count, seq_len, local_width).astype(jnp.bfloat16)
    partial_branch = jnp.einsum(
        "rsf,df->rsd", attended, out_full, preferred_element_type=jnp.float32
    )
    gain_two, shift_two, up_full, down_full = gather_turned(
        (norm2_gain, norm2_shift, w_up, w_down), "dp", (0, 0, 0, 0)
    )
    inputs_share = lax.dynamic_slice_in_dim(inputs, share_start, share_len, 1)
    middle = inputs_share + share_sum(partial_branch)
    normed_two, inv_two = standardize(middle)
    ffn_share = (normed_two * gain_two.astype(jnp.float32) + shift_two.astype(jnp.float32)).astype(
        jnp.bfloat16
    )
    ffn_in = gather_low(ffn_share)
    up_proj = jnp.einsum("rsd,df->rsf", ffn_in, up_full, preferred_element_type=jnp.float32)
    hidden = jax.nn.gelu(up_proj, approximate=True).astype(jnp.bfloat16)
    partial_ffn = jnp.einsum("rsf,df->rsd", hidden, down_full, preferred_element_type=jnp.float32)
    layer_out = middle + share_sum(partial_ffn)
    gain_two, shift_two, up_full, down_full = (gain_two, shift_two, up_full, down_full)
    grad_out = cotangent.astype(jnp.float32)
    grad_w_down = jnp.einsum("rsd,rsf->df", cotangent, hidden, preferred_element_type=jnp.float32)
    grad_hidden = jnp.einsum(
        "rsd,df->rsf", cotangent, down_full, preferred_element_type=jnp.float32
    )
    gelu_value, gelu_pull = jax.vjp(
        lambda arg_value: jax.nn.gelu(arg_value, approximate=True), up_proj
    )
    grad_up = gelu_pull(grad_hidden)[0].astype(jnp.bfloat16)
    grad_w_up = jnp.einsum("rsd,rsf->df", ffn_in, grad_up, preferred_element_type=jnp.float32)
    partial_ffn_in = jnp.einsum("rsf,df->rsd", grad_up, up_full, preferred_element_type=jnp.float32)
    grad_ffn_in = share_sum(partial_ffn_in)
    grad_out_part = lax.dynamic_slice_in_dim(grad_out, share_start, share_len, 1)
    grad_norm_mid, grad_gain_two, grad_shift_two = norm_back(
        grad_ffn_in, normed_two, inv_two, gain_two.astype(jnp.float32)
    )
    grad_middle = grad_out_part + grad_norm_mid
    grad_gain_two, grad_shift_two, grad_w_up, grad_w_down = (
        lax.psum_scatter(
            grad_gain_two.astype(jnp.bfloat16), "dp", scatter_dimension=0, tiled=True
        ).astype(jnp.float32),
        *tuple(
            (
                part.astype(jnp.float32)
                for part in in_one_piece(
                    (
                        grad_shift_two.astype(jnp.bfloat16),
                        grad_w_up.astype(jnp.bfloat16),
                        grad_w_down.astype(jnp.bfloat16),
                    ),
                    "dp",
                    0,
                    1,
                )
            )
        ),
    )
    gain_one, shift_one, qkv_full, out_full = (gain_one, shift_one, qkv_full, out_full)
    grad_branch = gather_low(grad_middle.astype(jnp.bfloat16))
    grad_w_out = jnp.einsum(
        "rsd,rsf->df", grad_branch, attended, preferred_element_type=jnp.float32
    )
    grad_attended = jnp.einsum(
        "rsd,df->rsf", grad_branch, out_full, preferred_element_type=jnp.float32
    ).astype(jnp.bfloat16)
    grad_att_heads = grad_attended.reshape(row_count, seq_len, local_heads, HEAD)
    again_scores = score_block(query_heads, key_heads, allowed)
    probs = jnp.exp(again_scores - log_total)
    probs_low = probs.astype(jnp.bfloat16)
    grad_probs = jnp.einsum(
        "rqhe,rkhe->rhqk", grad_att_heads, value_heads, preferred_element_type=jnp.float32
    )
    inner = jnp.sum(grad_probs * probs, axis=-1, keepdims=True)
    grad_scores = (probs * (grad_probs - inner)).astype(jnp.bfloat16)
    grad_query = jnp.einsum(
        "rhqk,rkhe->rqhe", grad_scores, key_heads, preferred_element_type=jnp.float32
    ) * HEAD ** (-0.5)
    grad_key = jnp.einsum(
        "rhqk,rqhe->rkhe", grad_scores, query_heads, preferred_element_type=jnp.float32
    ) * HEAD ** (-0.5)
    grad_value = jnp.einsum(
        "rhqk,rqhe->rkhe", probs_low, grad_att_heads, preferred_element_type=jnp.float32
    )
    grad_projected = (
        jnp.stack([grad_query, grad_key, grad_value])
        .reshape(3, row_count, seq_len, local_width)
        .astype(jnp.bfloat16)
    )
    grad_w_qkv = jnp.einsum(
        "rsd,trsf->dtf", attn_in, grad_projected, preferred_element_type=jnp.float32
    )
    partial_attn_in = jnp.einsum(
        "trsf,dtf->rsd", grad_projected, qkv_full, preferred_element_type=jnp.float32
    )
    grad_attn_in = share_sum(partial_attn_in)
    normed_part = lax.dynamic_slice_in_dim(normed_one, share_start, share_len, 1)
    inv_part = lax.dynamic_slice_in_dim(inv_one, share_start, share_len, 1)
    grad_norm_in, grad_gain_one, grad_shift_one = norm_back(
        grad_attn_in, normed_part, inv_part, gain_one.astype(jnp.float32)
    )
    input_grad = grad_middle + grad_norm_in
    grad_gain_one, grad_shift_one, grad_w_qkv, grad_w_out = (
        lax.psum_scatter(
            grad_gain_one.astype(jnp.bfloat16), "dp", scatter_dimension=0, tiled=True
        ).astype(jnp.float32),
        *tuple(
            (
                part.astype(jnp.float32)
                for part in in_one_piece(
                    (
                        grad_shift_one.astype(jnp.bfloat16),
                        grad_w_qkv.astype(jnp.bfloat16),
                        grad_w_out.astype(jnp.bfloat16),
                    ),
                    "dp",
                    0,
                    1,
                )
            )
        ),
    )
    layer_out, input_grad = tuple(
        (
            part.astype(jnp.float32)
            for part in in_one_piece_2(
                (layer_out.astype(jnp.bfloat16), input_grad.astype(jnp.bfloat16)), "mp", 1, 0
            )
        )
    )
    grad_gain_one, grad_shift_one, grad_gain_two, grad_shift_two = together(
        (grad_gain_one, grad_shift_one, grad_gain_two, grad_shift_two), "mp"
    )
    return (
        layer_out,
        input_grad,
        grad_gain_one,
        grad_shift_one,
        grad_w_qkv,
        grad_w_out,
        grad_gain_two,
        grad_shift_two,
        grad_w_up,
        grad_w_down,
    )


def solution(mesh):
    in_specs = (
        P("dp", None, None),
        P("dp", None),
        P("dp", None),
        P("dp", None),
        P(),
        P("dp"),
        P("dp"),
        P("dp", None, "mp"),
        P("dp", "mp"),
        P("dp"),
        P("dp"),
        P("dp", "mp"),
        P("dp", "mp"),
        P("dp", None, None),
    )
    out_specs = (
        P("dp", None, None),
        P("dp", None, None),
        P("dp"),
        P("dp"),
        P("dp", None, "mp"),
        P("dp", "mp"),
        P("dp"),
        P("dp"),
        P("dp", "mp"),
        P("dp", "mp"),
    )
    return jax.shard_map(
        on_device, mesh=mesh, in_specs=in_specs, out_specs=out_specs, check_vma=False
    )
```

profile of v0, /device:TPU:16, one launch (start us, length us, event | category | flops | bytes accessed | tf_op | source)
XLA Modules:
  0.0 1161.8 jit_solution(16425930208078286402)
XLA Ops:
  9.7 1.8 concatenate.26
  13.1 2.2 concatenate.27
  16.0 12.3 %gather_fusion = bf16[512,2048]{1,0:T(8,128)(2,1)S(1)} fusion(bf16[4096,2048]{1,0:T(8,128)(2,1)} %param.18, s32[1024]{0:T(1024)S(1)} %pad_clamp_fusion), kind=kCustom, calls=%fused_computation | custom fusion | bytes 4196352 | tf_op jit(solution)/shard_map/jit(_take)/gather | solution.py:147
  28.4 2.4 fusion.66
  32.8 2.5 subtract_multiply_fusion
  35.3 146.5 %all-gather.4.cloned.1.call-done = bf16[2048,2050]{1,0:T(8,128)(2,1)} async-done(((bf16[64,2050]{1,0:T(8,128)(2,1)}), bf16[2048,2050]{1,0:T(8,128)(2,1)}) %all-gather.4.cloned.1.call-update) | async-done | bytes 8396816 | tf_op jit(solution)/shard_map/all_gather | solution.py:45
  181.8 9.1 slice.86
  190.9 8.9 copy.125
  199.8 1.8 convert_reduce_fusion.3
  201.6 7.6 fusion.41
  212.4 5.8 convolution_bitcast_fusion.1
  218.2 6.0 all-to-all-start
  224.2 46.6 %all-to-all-done = f32[4,1,128,2048]{3,2,1,0:T(8,128)} async-done(((f32[4,1,128,2048]{3,2,1,0:T(8,128)}), f32[4,1,128,2048]{3,2,1,0:T(8,128)}, u32[]{:S(2)}, u32[]{:S(2)}) %all-to-all-start) | async-done | bytes 4194336 | tf_op jit(solution)/shard_map/all_to_all | solution.py:20
  270.8 2.6 reduce_sum.182
  275.1 105.4 %all-gather.6.cloned.1.call-done = bf16[2048,4098]{1,0:T(8,128)(2,1)} async-done(((bf16[64,4098]{1,0:T(8,128)(2,1)}), bf16[2048,4098]{1,0:T(8,128)(2,1)}) %all-gather.6.cloned.1.call-update) | async-done | bytes 16785424 | tf_op jit(solution)/shard_map/all_gather | solution.py:45
  382.8 29.3 %all_to_all.36 = bf16[4,1,128,2048]{3,2,1,0:T(8,128)(2,1)S(1)} all-to-all(bf16[4,1,128,2048]{3,2,1,0:T(8,128)(2,1)S(1)} %broadcast_in_dim.44), channel_id=1, replica_groups=mesh['dp'=32,'mp'=4] {'mp'}, dimensions={0} | all-to-all | bytes 4194304 | tf_op jit(solution)/shard_map/all_to_all | solution.py:26
  412.1 12.6 %multiply_convert_fusion.1 = (bf16[512,2048]{1,0:T(8,128)(2,1)}, f32[512,2048]{1,0:T(8,128)}) fusion(bf16[512,2048]{1,0:T(8,128)(2,1)S(1)} %bitcast.181, bf16[2048,4098]{1,0:T(8,128)(2,1)} %all-gather.6.cloned.1.call-done), kind=kOutput, calls=%fused_computation.31 | convolution fusion | flops 4304404480 | bytes 16777216 | tf_op jit(solution)/shard_map/rsd,df->rsf/dot_general | solution.py:185
  424.7 8.9 fusion.16
  435.0 6.3 fusion.24
  441.3 8.2 all-to-all-start.3
  449.5 10.8 fusion.21
  460.3 35.8 %all-to-all-done.3 = f32[4,1,128,2048]{3,2,1,0:T(8,128)} async-done(((f32[4,1,128,2048]{3,2,1,0:T(8,128)}), f32[4,1,128,2048]{3,2,1,0:T(8,128)}, u32[]{:S(2)}, u32[]{:S(2)}) %all-to-all-start.3) | async-done | bytes 4194336 | tf_op jit(solution)/shard_map/all_to_all | solution.py:20
  496.1 8.0 all-to-all-start.2
  504.1 2.8 fusion.64
  507.1 43.6 %all-to-all-done.2 = f32[4,1,128,2048]{3,2,1,0:T(8,128)} async-done(((f32[4,1,128,2048]{3,2,1,0:T(8,128)}), f32[4,1,128,2048]{3,2,1,0:T(8,128)}, u32[]{:S(2)}, u32[]{:S(2)}) %all-to-all-start.2) | async-done | bytes 4194336 | tf_op jit(solution)/shard_map/all_to_all | solution.py:20
  550.7 3.6 reduce_sum.186
  554.2 2.4 fusion.52
  556.6 2.5 convert_bitcast_fusion.1
  560.7 7.0 all-to-all-start.4
  567.7 24.0 %all-to-all-done.4 = bf16[4,1,128,2048]{3,2,1,0:T(8,128)(2,1)S(1)} async-done(((bf16[4,1,128,2048]{3,2,1,0:T(8,128)(2,1)}), bf16[4,1,128,2048]{3,2,1,0:T(8,128)(2,1)S(1)}, u32[]{:S(2)}, u32[]{:S(2)}) %all-to-all-start.4) | async-done | bytes 2097184 | tf_op jit(solution)/shard_map/all_to_all | solution.py:26
  591.7 4.5 fusion.42
  603.2 8.7 convolution_bitcast_fusion
  611.9 8.0 all-to-all-start.5
  620.0 46.5 %all-to-all-done.5 = f32[4,1,128,2048]{3,2,1,0:T(8,128)} async-done(((f32[4,1,128,2048]{3,2,1,0:T(8,128)}), f32[4,1,128,2048]{3,2,1,0:T(8,128)}, u32[]{:S(2)}, u32[]{:S(2)}) %all-to-all-start.5) | async-done | bytes 4194336 | tf_op jit(solution)/shard_map/all_to_all | solution.py:20
  666.5 3.0 fusion.63
  671.8 3.6 convolution_convert_fusion.2
  675.4 3.2 copy.145
  678.6 8.4 convolution_convert_fusion.1
  687.0 8.6 copy.144
  696.0 15.5 %concatenate.29 = bf16[2048,2049]{1,0:T(8,128)(2,1)} concatenate(bf16[2048,1]{1,0:T(8,128)(2,1)S(1)} %convert_element_type.270, bf16[2048,1536]{1,0:T(8,128)(2,1)} %copy.144, bf16[2048,512]{1,0:T(8,128)(2,1)S(1)} %copy.145), dimensions={1} | concatenate | bytes 16785408 | tf_op jit(solution)/shard_map/concatenate | solution.py:55
  713.1 8.6 convolution_convert_fusion
  721.6 6.9 convert_bitcast_fusion
  728.6 82.1 %concatenate.30 = bf16[2048,4097]{0,1:T(8,128)(2,1)} concatenate(bf16[2048,1]{0,1:T(2,128)(2,1)S(1)} %convert_element_type.255, bf16[2048,2048]{0,1:T(8,128)(2,1)} %convolution_convert_fusion, bf16[2048,2048]{0,1:T(8,128)(2,1)} %convert_bitcast_fusion), dimensions={1} | concatenate | bytes 33562624 | tf_op jit(solution)/shard_map/concatenate | solution.py:55
  810.7 21.4 %copy.161 = bf16[2048,4097]{1,0:T(8,128)(2,1)} copy(bf16[2048,4097]{0,1:T(8,128)(2,1)} %concatenate.30) | data formatting | bytes 33562624
  834.0 122.2 %all-reduce.2 = (bf16[2048]{0:T(1024)(128)(2,1)S(1)}, bf16[2048]{0:T(1024)(128)(2,1)S(1)}) all-reduce(bf16[2048]{0:T(1024)(128)(2,1)S(1)} %get-tuple-element.70, bf16[2048]{0:T(1024)(128)(2,1)S(1)} %get-tuple-element.64), channel_id=4, replica_groups=mesh['dp'=32,'mp'=4] {'dp'}, use_global_device_ids=true, to_apply=%region_20.21.clone | all-reduce | flops 4096 | bytes 16384
  956.3 6.7 slice_convert_fusion
  967.4 176.7 %reduce-scatter.7.cloned.1.call-done = bf16[64,4097]{1,0:T(8,128)(2,1)} async-done(((bf16[2048,4097]{1,0:T(8,128)(2,1)}), bf16[64,4097]{1,0:T(8,128)(2,1)}) %reduce-scatter.7.cloned.1.call-update) | async-done | bytes 524432
  1145.6 4.8 all-to-all-start.6
  (136 shorter events, 39.7 us)
Async XLA Ops:
  7.2 174.7 %all-gather.4.cloned.1.call-start = ((), (), s32[]{:S(2)}) async-start(), calls=%async_computation.9 | async-start | bytes 9191424 | tf_op jit(solution)/shard_map/all_gather | solution.py:45
  11.5 369.0 %all-gather.6.cloned.1.call-start = ((), (), s32[]{:S(2)}) async-start(), calls=%async_computation.10 | async-start | bytes 17842176 | tf_op jit(solution)/shard_map/all_gather | solution.py:45
  16.0 12.4 %copy-start.21 = (s32[1,512]{1,0:T(1,128)S(1)}, s32[1,512]{1,0:T(1,128)}, u32[]{:S(2)}) copy-start(s32[1,512]{1,0:T(1,128)} %param.17) | copy-start | bytes 6148
  30.8 2.0 copy-start.2
  30.9 0.7 copy-start.20
  209.3 1.6 copy-start.9
  210.3 2.0 copy-start
  212.2 5.9 copy-start.17
  218.2 52.6 %all-to-all-start = ((f32[4,1,128,2048]{3,2,1,0:T(8,128)}), f32[4,1,128,2048]{3,2,1,0:T(8,128)}, u32[]{:S(2)}, u32[]{:S(2)}) async-start(f32[4,1,128,2048]{3,2,1,0:T(8,128)} %convolution_bitcast_fusion.1), calls=%async_computation | async-start | bytes 8388608 | tf_op jit(solution)/shard_map/all_to_all | solution.py:20
  382.7 41.9 %slice-start = ((s8[17301504]{0:T(1024)(128)(4,1)}), s8[4194304]{0:T(1024)(128)(4,1)S(1)}, s32[]{:S(2)}) async-start(s8[17301504]{0:T(1024)(128)(4,1)} %bitcast.200), calls=%async_computation.14 | async-start | bytes 8388608
  412.0 12.6 %copy-start.5 = (bf16[4,1,128,2048]{3,2,1,0:T(8,128)(2,1)}, bf16[4,1,128,2048]{3,2,1,0:T(8,128)(2,1)S(1)}, u32[]{:S(2)}) copy-start(bf16[4,1,128,2048]{3,2,1,0:T(8,128)(2,1)S(1)} %all_to_all.36) | copy-start | bytes 6291460
  412.0 12.6 %copy-start.18 = (bf16[1,512,2048]{2,1,0:T(8,128)(2,1)S(1)}, bf16[1,512,2048]{2,1,0:T(8,128)(2,1)}, u32[]{:S(2)}) copy-start(bf16[1,512,2048]{2,1,0:T(8,128)(2,1)} %param.27) | copy-start | bytes 6291460
  412.0 12.6 %slice-start.1 = ((s8[17301504]{0:T(1024)(128)(4,1)}), s8[4194304]{0:T(1024)(128)(4,1)S(1)}, s32[]{:S(2)}) async-start(s8[17301504]{0:T(1024)(128)(4,1)} %bitcast.200), calls=%async_computation.15 | async-start | bytes 8388608
  412.1 12.7 %slice-start.2 = ((s8[17301504]{0:T(1024)(128)(4,1)}), s8[4194304]{0:T(1024)(128)(4,1)S(1)}, s32[]{:S(2)}) async-start(s8[17301504]{0:T(1024)(128)(4,1)} %bitcast.200), calls=%async_computation.16 | async-start | bytes 8388608
  412.1 12.7 %slice-start.3 = ((s8[17301504]{0:T(1024)(128)(4,1)}), s8[4194304]{0:T(1024)(128)(4,1)S(1)}, s32[]{:S(2)}) async-start(s8[17301504]{0:T(1024)(128)(4,1)} %bitcast.200), calls=%async_computation.17 | async-start | bytes 8388608
  412.1 12.7 %slice-start.4 = ((s8[17301504]{0:T(1024)(128)(4,1)}), s8[524288]{0:T(1024)(128)(4,1)S(1)}, s32[]{:S(2)}) async-start(s8[17301504]{0:T(1024)(128)(4,1)} %bitcast.200), calls=%async_computation.18 | async-start | bytes 1048576
  433.7 1.3 copy-start.23
  441.3 54.8 %all-to-all-start.3 = ((f32[4,1,128,2048]{3,2,1,0:T(8,128)}), f32[4,1,128,2048]{3,2,1,0:T(8,128)}, u32[]{:S(2)}, u32[]{:S(2)}) async-start(f32[4,1,128,2048]{3,2,1,0:T(8,128)} %fusion.24), calls=%async_computation.3 | async-start | bytes 8388608 | tf_op jit(solution)/shard_map/all_to_all | solution.py:20
  496.1 54.6 %all-to-all-start.2 = ((f32[4,1,128,2048]{3,2,1,0:T(8,128)}), f32[4,1,128,2048]{3,2,1,0:T(8,128)}, u32[]{:S(2)}, u32[]{:S(2)}) async-start(f32[4,1,128,2048]{3,2,1,0:T(8,128)} %fusion.21), calls=%async_computation.2 | async-start | bytes 8388608 | tf_op jit(solution)/shard_map/all_to_all | solution.py:20
  560.7 31.0 %all-to-all-start.4 = ((bf16[4,1,128,2048]{3,2,1,0:T(8,128)(2,1)}), bf16[4,1,128,2048]{3,2,1,0:T(8,128)(2,1)S(1)}, u32[]{:S(2)}, u32[]{:S(2)}) async-start(bf16[4,1,128,2048]{3,2,1,0:T(8,128)(2,1)} %broadcast_in_dim.46), calls=%async_computation.4 | async-start | bytes 4194304 | tf_op jit(solution)/shard_map/all_to_all | solution.py:26
  591.7 5.4 copy-start.7
  591.7 4.5 copy-start.1
  596.2 1.0 copy-start.10
  597.2 3.4 copy-start.12
  600.2 3.0 copy-start.14
  600.6 0.8 copy-start.16
  611.9 54.6 %all-to-all-start.5 = ((f32[4,1,128,2048]{3,2,1,0:T(8,128)}), f32[4,1,128,2048]{3,2,1,0:T(8,128)}, u32[]{:S(2)}, u32[]{:S(2)}) async-start(f32[4,1,128,2048]{3,2,1,0:T(8,128)} %convolution_bitcast_fusion), calls=%async_computation.5 | async-start | bytes 8388608 | tf_op jit(solution)/shard_map/all_to_all | solution.py:20
  619.9 336.4 %all-gather.8.cloned.1.call-start = ((), (), s32[]{:S(2)}) async-start(), calls=%async_computation.11 | async-start | bytes 5242880 | tf_op jit(solution)/shard_map/all_gather | solution.py:67
  620.0 50.3 %copy-start.4 = (f32[1,128,2048]{2,1,0:T(8,128)S(1)}, f32[1,128,2048]{2,1,0:T(8,128)}, u32[]{:S(2)}) copy-start(f32[1,128,2048]{2,1,0:T(8,128)} %get-tuple-element.75) | copy-start | bytes 3145732
  666.5 3.4 copy-start.3
  669.6 1.0 copy-start.11
  670.0 1.8 copy-start.8
  671.7 291.3 %reduce-scatter.5.cloned.1.call-start = ((), (), s32[]{:S(2)}) async-start(), calls=%async_computation.12 | async-start | bytes 9191424 | tf_op jit(solution)/shard_map/reduce_scatter | solution.py:56
  675.4 3.2 copy-start.13
  675.4 3.2 copy-start.15
  711.5 1.6 copy-start.6
  711.5 432.6 %reduce-scatter.7.cloned.1.call-start = ((), (), s32[]{:S(2)}) async-start(), calls=%async_computation.13 | async-start | bytes 17842176
  713.0 8.6 copy-start.19
  713.1 8.6 copy-start.22
  832.1 0.7 copy-start.24
  1145.6 8.6 all-to-all-start.6
Sparse Core Ops, SparseCore 0:
  11.6 170.1 all-gather.3
  183.5 196.9 all-gather.5
  671.8 80.5 all-gather.7
  754.7 183.4 reduce-scatter.4
  940.5 203.5 reduce-scatter.6
where the time goes:
time: 1180 us; the launch traced here: 1160 us
  waiting for transfers between devices  625 us (53%)
  local copies, waits for them, and re-layouts  188 us (16%)
  blocking collectives  151 us (13%)
  matrix products  97.7 us (8%)
  other arithmetic  42.4 us (4%)
  starting transfers between devices  42.1 us (4%)
  between operations  15.4 us (1%)
    all_gather x2, waiting for transfers between devices, gather_turned(): filled, at, done = (lax.all_gather(both, axis, axis=0, tiled=True), 0, [])  252 us
    unnamed x6, waiting for transfers between devices  177 us
    all_to_all x4, waiting for transfers between devices, sent_and_summed(): lax.all_to_all(pieces, axis, split_axis=0, concat_axis=0, tiled=True)  173 us
    unnamed x1, blocking collectives  122 us
    concatenate x2, local copies, waits for them, and re-layouts, in_one_piece(): both = jnp.concatenate(columns, axis=along)  97.6 us
    unnamed x69, local copies, waits for them, and re-layouts  31.1 us
    all_to_all x4, starting transfers between devices, sent_and_summed(): lax.all_to_all(pieces, axis, split_axis=0, concat_axis=0, tiled=True)  30.2 us
    all_to_all x1, blocking collectives, from_everyone(): lax.all_to_all(jnp.broadcast_to(value[None], (peers, *value.shape)), axis...  29.3 us
  transfers between devices with their start and end apart: 11, of which 8 were waited for; matrix products, arithmetic and copies ran while one was open for 22% of the time, Pallas kernels for 0%

commit v1 on v0

v1 whole, which is shorter than its diff:
```python
import functools

import jax
import jax.numpy as jnp
from jax import lax
from jax.experimental import pallas as pl
from jax.experimental.pallas import tpu as pltpu
from jax.sharding import PartitionSpec as P

HEAD = 128
WIDTH = 2048
SHARE = 128
PART = 1024
MESH = pl.DeviceIdType.MESH
ANY = pl.BlockSpec(memory_space=pl.ANY)
VMEM = pl.BlockSpec(memory_space=pltpu.VMEM)
masked_score = -1000000000.0
epsilon = 1e-05
f32 = jnp.float32
bf16 = jnp.bfloat16


def place():
    dp, mp = lax.axis_index("dp"), lax.axis_index("mp")
    return lax.div(dp, 16), lax.rem(lax.div(dp, 4), 4), lax.rem(dp, 4), lax.div(mp, 2), lax.rem(mp, 2)


def ring(position, step):
    return lax.rem(position + step + 4, 4)


def xz_neighbour(axis, step):
    ylo, x, z, yhi, core = place()
    if axis == 0:
        x = ring(x, step)
    else:
        z = ring(z, step)
    return (ylo * 16 + x * 4 + z, yhi * 2 + core)


def y_peer(step):
    ylo, x, z, yhi, core = place()
    y = ring(yhi * 2 + ylo, step)
    return (lax.rem(y, 2) * 16 + x * 4 + z, lax.div(y, 2) * 2 + core)


def lo_partner():
    ylo, x, z, yhi, core = place()
    return ((1 - ylo) * 16 + x * 4 + z, yhi * 2 + core)


def core_partner():
    ylo, x, z, yhi, core = place()
    return (ylo * 16 + x * 4 + z, yhi * 2 + 1 - core)


def greet(peers):
    barrier = pltpu.get_barrier_semaphore()
    for peer in peers:
        pl.semaphore_signal(barrier, inc=1, device_id=peer, device_id_type=MESH)
    pl.semaphore_wait(barrier, len(peers))


def remote(src, dst, send_sem, recv_sem, peer):
    return pltpu.make_async_remote_copy(
        src_ref=src,
        dst_ref=dst,
        send_sem=send_sem,
        recv_sem=recv_sem,
        device_id=peer,
        device_id_type=MESH,
    )


def sems(*shape):
    return pltpu.SemaphoreType.DMA(shape)


def params(collective_id, mib=48):
    return pltpu.CompilerParams(
        collective_id=collective_id, has_side_effects=True, vmem_limit_bytes=mib << 20
    )


def small_gather_kernel(own, mask, everyone, mask_out, send, recv, mask_send, mask_recv):
    dp, mp = lax.axis_index("dp"), lax.axis_index("mp")
    barrier = pltpu.get_barrier_semaphore()

    def greet_one(k, carry):
        pl.semaphore_signal(
            barrier, inc=1, device_id=(lax.rem(dp + k, 32), mp), device_id_type=MESH
        )
        return carry

    lax.fori_loop(1, 32, greet_one, 0)
    pl.semaphore_wait(barrier, 31)

    def move(k):
        peer = lax.rem(dp + k, 32)
        return remote(own, everyone.at[dp], send.at[k], recv.at[dp], (peer, mp))

    def start(k, carry):
        move(k).start()
        return carry

    def finish(k, carry):
        source = lax.rem(dp + k, 32)
        move(k).wait_send()
        remote(own, everyone.at[source], send.at[k], recv.at[source], (source, mp)).wait_recv()
        return carry

    swap = remote(mask, mask_out, mask_send, mask_recv, lo_partner())
    swap.start()
    lax.fori_loop(1, 32, start, 0)
    everyone[dp] = own[...]
    lax.fori_loop(1, 32, finish, 0)
    swap.wait()


def small_gather(own, mask, collective_id):
    return pl.pallas_call(
        small_gather_kernel,
        out_shape=(
            jax.ShapeDtypeStruct((32, 8, 128), f32),
            jax.ShapeDtypeStruct((8, 128), f32),
        ),
        in_specs=[VMEM, VMEM],
        out_specs=(VMEM, VMEM),
        scratch_shapes=[sems(32), sems(32), pltpu.SemaphoreType.DMA, pltpu.SemaphoreType.DMA],
        compiler_params=params(collective_id, 8),
    )(own, mask)


def small_reduce_kernel(pieces, out, arrived, summed, more, send, recv, send_two, recv_two):
    dp, mp = lax.axis_index("dp"), lax.axis_index("mp")
    barrier = pltpu.get_barrier_semaphore()

    def greet_one(k, carry):
        pl.semaphore_signal(
            barrier, inc=1, device_id=(lax.rem(dp + k, 32), mp), device_id_type=MESH
        )
        return carry

    lax.fori_loop(1, 32, greet_one, 0)
    for k in (1, 2, 3):
        pl.semaphore_signal(
            barrier, inc=1, device_id=(dp, lax.rem(mp + k, 4)), device_id_type=MESH
        )
    pl.semaphore_wait(barrier, 34)

    def move(k):
        peer = lax.rem(dp + k, 32)
        return remote(pieces.at[peer], arrived.at[k], send.at[k], recv.at[k], (peer, mp))

    def start(k, carry):
        move(k).start()
        return carry

    def finish(k, total):
        move(k).wait()
        return total + arrived[k]

    lax.fori_loop(1, 32, start, 0)
    summed[...] = lax.fori_loop(1, 32, finish, pieces[dp])
    copies = [
        remote(summed, more.at[k - 1], send_two.at[k], recv_two.at[k], (dp, lax.rem(mp + k, 4)))
        for k in (1, 2, 3)
    ]
    for copy in copies:
        copy.start()
    for copy in copies:
        copy.wait()
    out[...] = summed[...] + more[0] + more[1] + more[2]


def small_reduce(pieces, collective_id):
    return pl.pallas_call(
        small_reduce_kernel,
        out_shape=jax.ShapeDtypeStruct((8, 128), f32),
        in_specs=[VMEM],
        out_specs=VMEM,
        scratch_shapes=[
            pltpu.VMEM((32, 8, 128), f32),
            pltpu.VMEM((8, 128), f32),
            pltpu.VMEM((3, 8, 128), f32),
            sems(32),
            sems(32),
            sems(4),
            sems(4),
        ],
        compiler_params=params(collective_id, 8),
    )(pieces)


def row_exchange_kernel(count, halves, full, local_sem, send, recv):
    ylo, x, z, yhi, core = place()
    up, down, other = y_peer(1), y_peer(-1), core_partner()
    greet([up, down, other])
    first = []
    for n in range(count):
        first.append(remote(halves.at[n, 0], full.at[n, ylo, core, 0], send.at[n, 0], recv.at[n, 0], up))
        first.append(remote(halves.at[n, 1], full.at[n, ylo, core, 1], send.at[n, 1], recv.at[n, 1], down))
    for n in range(count):
        first.append(remote(halves.at[n], full.at[n, ylo, core], send.at[n, 2], recv.at[n, 2], other))
    for copy in first:
        copy.start()
    local = [pltpu.make_async_copy(halves.at[n], full.at[n, ylo, core], local_sem.at[n]) for n in range(count)]
    for copy in local:
        copy.start()
    second = []
    for n in range(count):
        for u in range(2):
            here = full.at[n, 1 - ylo, core, u]
            remote(halves.at[n, u], here, send.at[n, u], recv.at[n, u], up).wait_recv()
            copy = remote(here, here, send.at[n, 3 + u], recv.at[n, 3 + u], other)
            copy.start()
            second.append(copy)
    for n in range(count):
        remote(halves.at[n], full.at[n, ylo, 1 - core], send.at[n, 2], recv.at[n, 2], other).wait_recv()
        for u in range(2):
            here = full.at[n, 1 - ylo, 1 - core, u]
            remote(here, here, send.at[n, 3 + u], recv.at[n, 3 + u], other).wait_recv()
    for copy in first + second:
        copy.wait_send()
    for copy in local:
        copy.wait()


def row_exchange(halves, collective_id):
    count = halves.shape[0]
    return pl.pallas_call(
        functools.partial(row_exchange_kernel, count),
        out_shape=jax.ShapeDtypeStruct((count, 2, 2, 2, SHARE, WIDTH), bf16),
        in_specs=[ANY],
        out_specs=ANY,
        scratch_shapes=[sems(count), sems(count, 5), sems(count, 5)],
        compiler_params=params(collective_id),
    )(halves)


def share_gather_kernel(share, full, local_sem, send, recv):
    ylo, x, z, yhi, core = place()
    y = yhi * 2 + ylo
    other = core_partner()
    greet([y_peer(1), y_peer(2), y_peer(3), other])
    mine = full.at[ylo, core, yhi]
    local = pltpu.make_async_copy(share, mine, local_sem)
    local.start()
    first = [remote(share, mine, send.at[k], recv.at[k], y_peer(k) if k else other) for k in (2, 1, 3, 0)]
    for copy in first:
        copy.start()
    second = []
    for k in (1, 3, 2):
        source = ring(y, -k)
        here = full.at[lax.rem(source, 2), core, lax.div(source, 2)]
        remote(share, here, send.at[k], recv.at[k], y_peer(-k)).wait_recv()
        copy = remote(here, here, send.at[3 + k], recv.at[3 + k], other)
        copy.start()
        second.append(copy)
    remote(share, full.at[ylo, 1 - core, yhi], send.at[0], recv.at[0], other).wait_recv()
    for k in (1, 3, 2):
        source = ring(y, -k)
        here = full.at[lax.rem(source, 2), 1 - core, lax.div(source, 2)]
        remote(here, here, send.at[3 + k], recv.at[3 + k], other).wait_recv()
    for copy in first + second:
        copy.wait_send()
    local.wait()


def share_gather(share, collective_id):
    return pl.pallas_call(
        share_gather_kernel,
        out_shape=jax.ShapeDtypeStruct((2, 2, 2, SHARE, WIDTH), bf16),
        in_specs=[ANY],
        out_specs=ANY,
        scratch_shapes=[pltpu.SemaphoreType.DMA, sems(7), sems(7)],
        compiler_params=params(collective_id),
    )(share)


CHUNK = 16


def share_sum_kernel(partial, out, from_core, turned, arrived, send, recv, send_two, recv_two):
    ylo, x, z, yhi, core = place()
    y = yhi * 2 + ylo
    other = core_partner()
    greet([y_peer(1), y_peer(2), y_peer(3), other])

    def block(k, half):
        target = ring(y, k)
        return partial.at[lax.rem(target, 2), half, lax.div(target, 2)]

    first = {}
    for k in (2, 1, 3, 0):
        first[k] = remote(block(k, 1 - core), from_core.at[k], send.at[k], recv.at[k], other)
        first[k].start()
    second = {}
    for k in (2, 1, 3):
        first[k].wait_recv()
        mine = block(k, core)

        def add(i, carry):
            rows = pl.ds(pl.multiple_of(i * CHUNK, CHUNK), CHUNK)
            turned[k, rows] = (mine[rows].astype(f32) + from_core[k, rows].astype(f32)).astype(bf16)
            return carry

        lax.fori_loop(0, SHARE // CHUNK, add, 0)
        second[k] = remote(turned.at[k], arrived.at[k], send_two.at[k], recv_two.at[k], y_peer(k))
        second[k].start()
    first[0].wait_recv()
    for k in (1, 3, 2):
        second[k].wait_recv()
    mine_own = block(0, core)

    def total(i, carry):
        rows = pl.ds(pl.multiple_of(i * CHUNK, CHUNK), CHUNK)
        value = mine_own[rows].astype(f32) + from_core[0, rows].astype(f32)
        for k in (1, 2, 3):
            value += arrived[k, rows].astype(f32)
        out[rows] = value
        return carry

    lax.fori_loop(0, SHARE // CHUNK, total, 0)
    for k in range(4):
        first[k].wait_send()
    for k in (1, 2, 3):
        second[k].wait_send()


def share_sum(partial, collective_id):
    return pl.pallas_call(
        share_sum_kernel,
        out_shape=jax.ShapeDtypeStruct((SHARE, WIDTH), f32),
        in_specs=[VMEM],
        out_specs=VMEM,
        scratch_shapes=[
            pltpu.VMEM((4, SHARE, WIDTH), bf16),
            pltpu.VMEM((4, SHARE, WIDTH), bf16),
            pltpu.VMEM((4, SHARE, WIDTH), bf16),
            sems(4),
            sems(4),
            sems(4),
            sems(4),
        ],
        compiler_params=params(collective_id),
    )(partial.reshape(2, 2, 2, SHARE, WIDTH))


def row_gather_kernel(share, full, local_sem, send, recv):
    ylo, x, z, yhi, core = place()
    across, other = y_peer(2), core_partner()
    greet([across, other])
    mine = full.at[:, core, yhi]
    far = full.at[:, core, 1 - yhi]
    local = pltpu.make_async_copy(share, mine, local_sem)
    local.start()
    one = remote(share, mine, send.at[0], recv.at[0], across)
    two = remote(share, mine, send.at[1], recv.at[1], other)
    one.start()
    two.start()
    remote(share, far, send.at[0], recv.at[0], across).wait_recv()
    three = remote(far, far, send.at[2], recv.at[2], other)
    three.start()
    remote(share, full.at[:, 1 - core, yhi], send.at[1], recv.at[1], other).wait_recv()
    last = full.at[:, 1 - core, 1 - yhi]
    remote(last, last, send.at[2], recv.at[2], other).wait_recv()
    for copy in (one, two, three):
        copy.wait_send()
    local.wait()


def row_gather(share, collective_id):
    count = share.shape[0]
    return pl.pallas_call(
        row_gather_kernel,
        out_shape=jax.ShapeDtypeStruct((count, 2, 2, SHARE, WIDTH), bf16),
        in_specs=[ANY],
        out_specs=ANY,
        scratch_shapes=[pltpu.SemaphoreType.DMA, sems(3), sems(3)],
        compiler_params=params(collective_id),
    )(share)


SIGNS = (1, -1)


def weight_gather_kernel(own, full, local_sem, swap_send, swap_recv, send, recv):
    ylo, x, z, yhi, core = place()
    partner = lo_partner()
    near = [[xz_neighbour(axis, d) for d in SIGNS] for axis in (0, 1)]
    greet([partner] + near[0] + near[1])
    here = (x, z)
    arrays = own.shape[0]

    def number(s, r, stage, d):
        return ((s * 2 + r) * 4 + stage) * 2 + d

    def move(src, dst, s, r, stage, d, axis):
        n = number(s, r, stage, d)
        return remote(src, dst, send.at[n], recv.at[n], near[axis][d])

    def locate(s):
        a, o = lax.div(s, 2), lax.rem(s, 2)
        return a, ylo + o - 2 * o * ylo

    def block(s, r, step, rows):
        a, yl = locate(s)
        if r == 0:
            return full.at[a, yl, ring(x, step), z, rows]
        return full.at[a, yl, x, ring(z, step), rows]

    def line(s, r, step, part):
        a, yl = locate(s)
        if r == 0:
            return full.at[a, yl, part, ring(z, step), pl.ds(0, 32)]
        return full.at[a, yl, ring(x, step), part, pl.ds(32, 32)]

    def local(a):
        return pltpu.make_async_copy(own.at[a, ylo], full.at[a, ylo, x, z], local_sem.at[a])

    def swap(a):
        return remote(own.at[a, 1 - ylo], full.at[a, ylo, x, z], swap_send.at[a], swap_recv.at[a], partner)

    def swap_arrived(a):
        return remote(own.at[a, 1 - ylo], full.at[a, 1 - ylo, x, z], swap_send.at[a], swap_recv.at[a], partner)

    def begin(a, carry):
        swap(a).start()
        local(a).start()
        for r in range(2):
            rows = pl.ds(32 * r, 32)
            for d in range(2):
                move(own.at[a, ylo, rows], block(2 * a, r, 0, rows), 2 * a, r, 0, d, r).start()
        return carry

    lax.fori_loop(0, arrays, begin, 0)

    def begin_other(a, carry):
        swap_arrived(a).wait_recv()
        for r in range(2):
            rows = pl.ds(32 * r, 32)
            for d in range(2):
                mine = block(2 * a + 1, r, 0, rows)
                move(mine, mine, 2 * a + 1, r, 0, d, r).start()
        return carry

    lax.fori_loop(0, arrays, begin_other, 0)

    def forward(s, carry):
        for r in range(2):
            for d in range(2):
                rows = pl.ds(32 * r, 32)
                came = block(s, r, -SIGNS[d], rows)
                move(came, came, s, r, 0, d, r).wait_recv()
                piece = block(s, r, -SIGNS[d], pl.ds(32 * r + 16 * d, 16))
                move(piece, piece, s, r, 1, d, r).start()
        return carry

    lax.fori_loop(0, 2 * arrays, forward, 0)

    def wait_local(a, carry):
        local(a).wait()
        return carry

    lax.fori_loop(0, arrays, wait_local, 0)

    def lines(s, carry):
        for r in range(2):
            for d in range(2):
                piece = block(s, r, 2, pl.ds(32 * r + 16 * d, 16))
                move(piece, piece, s, r, 1, d, r).wait_recv()
            for d in range(2):
                mine = line(s, r, 0, slice(None))
                move(mine, mine, s, r, 2, d, 1 - r).start()
        return carry

    lax.fori_loop(0, 2 * arrays, lines, 0)

    def forward_lines(s, carry):
        for r in range(2):
            for d in range(2):
                came = line(s, r, -SIGNS[d], slice(None))
                move(came, came, s, r, 2, d, 1 - r).wait_recv()
                piece = line(s, r, -SIGNS[d], pl.ds(2 * d, 2))
                move(piece, piece, s, r, 3, d, 1 - r).start()
        return carry

    lax.fori_loop(0, 2 * arrays, forward_lines, 0)

    def finish(s, carry):
        for r in range(2):
            for d in range(2):
                piece = line(s, r, 2, pl.ds(2 * d, 2))
                move(piece, piece, s, r, 3, d, 1 - r).wait_recv()
                rows = pl.ds(32 * r, 32)
                mine = block(s, r, 0, rows)
                move(mine, mine, s, r, 0, d, r).wait_send()
                piece = block(s, r, -SIGNS[d], pl.ds(32 * r + 16 * d, 16))
                move(piece, piece, s, r, 1, d, r).wait_send()
                mine = line(s, r, 0, slice(None))
                move(mine, mine, s, r, 2, d, 1 - r).wait_send()
                piece = line(s, r, -SIGNS[d], pl.ds(2 * d, 2))
                move(piece, piece, s, r, 3, d, 1 - r).wait_send()
        return carry

    lax.fori_loop(0, 2 * arrays, finish, 0)

    def finish_swap(a, carry):
        swap(a).wait_send()
        return carry

    lax.fori_loop(0, arrays, finish_swap, 0)


def weight_gather(own, collective_id):
    arrays = own.shape[0]
    return pl.pallas_call(
        weight_gather_kernel,
        out_shape=jax.ShapeDtypeStruct((arrays, 2, 4, 4, 64, PART), bf16),
        in_specs=[ANY],
        out_specs=ANY,
        scratch_shapes=[sems(arrays), sems(arrays), sems(arrays), sems(arrays * 32), sems(arrays * 32)],
        compiler_params=params(collective_id),
    )(own)


def add_rows(count, one):
    def body(i, carry):
        one(pl.ds(pl.multiple_of(i * 16, 16), 16))
        return carry

    lax.fori_loop(0, count // 16, body, 0)


def weight_sum_kernel(
    grads, out, wide, wide_out, middle, thin, thin_out, total, swap_send, swap_recv, send, recv
):
    ylo, x, z, yhi, core = place()
    partner = lo_partner()
    near = [[xz_neighbour(axis, d) for d in SIGNS] for axis in (0, 1)]
    greet([partner] + near[0] + near[1])
    streams = grads.shape[0] * 2

    def number(s, r, stage, d):
        return ((s * 2 + r) * 6 + stage) * 2 + d

    def move(src, dst, s, r, stage, d, axis):
        n = number(s, r, stage, d)
        return remote(src, dst, send.at[n], recv.at[n], near[axis][d])

    def line(s, r, step, part):
        a, yl = lax.div(s, 2), lax.rem(s, 2)
        if r == 0:
            return grads.at[a, yl, part, ring(z, step), pl.ds(0, 32)]
        return grads.at[a, yl, ring(x, step), part, pl.ds(32, 32)]

    def at(r):
        return x if r == 0 else z

    def wide_move(s, r, d, kind):
        if kind == 0:
            src = line(s, r, 2, pl.ds(2 * d, 2))
        elif kind == 1:
            src = line(s, r, SIGNS[d], pl.ds(2 - 2 * d, 2))
        else:
            src = wide_out.at[s, r, d]
        return move(src, wide.at[s, r, kind, d], s, r, kind, d, 1 - r)

    def thin_move(s, r, d, kind):
        if kind == 0:
            src = middle.at[s, r, ring(at(r), 2), pl.ds(16 * d, 16)]
        elif kind == 1:
            src = middle.at[s, r, ring(at(r), SIGNS[d]), pl.ds(16 - 16 * d, 16)]
        else:
            src = thin_out.at[s, r, d]
        return move(src, thin.at[s, r, kind, d], s, r, 3 + kind, d, r)

    def step_one(s, carry):
        for r in range(2):
            for d in range(2):
                wide_move(s, r, d, 0).start()
        for r in range(2):
            for d in range(2):
                wide_move(s, r, d, 1).start()
        return carry

    lax.fori_loop(0, streams, step_one, 0)

    def step_two(s, carry):
        for r in range(2):
            for d in range(2):
                wide_move(s, r, d, 0).wait_recv()
                for p in range(2):
                    mine = line(s, r, SIGNS[d], 2 * d + p)

                    def one(rows):
                        wide_out[s, r, d, p, rows] = (
                            mine[rows].astype(f32) + wide[s, r, 0, d, p, rows].astype(f32)
                        ).astype(bf16)

                    add_rows(32, one)
                wide_move(s, r, d, 2).start()
        return carry

    lax.fori_loop(0, streams, step_two, 0)

    def step_three(s, carry):
        for r in range(2):
            for d in range(2):
                wide_move(s, r, d, 1).wait_recv()
                wide_move(s, r, d, 2).wait_recv()
            for p in range(4):
                mine = line(s, r, 0, p)
                d = p // 2

                def one(rows):
                    value = mine[rows].astype(f32) + wide[s, r, 2, d, p % 2, rows].astype(f32)
                    value += wide[s, r, 1, 1 - d, p % 2, rows].astype(f32)
                    middle[s, r, p, rows] = value.astype(bf16)

                add_rows(32, one)
            for d in range(2):
                thin_move(s, r, d, 0).start()
            for d in range(2):
                thin_move(s, r, d, 1).start()
        return carry

    lax.fori_loop(0, streams, step_three, 0)

    def step_four(s, carry):
        for r in range(2):
            for d in range(2):
                thin_move(s, r, d, 0).wait_recv()
                mine = middle[s, r, ring(at(r), SIGNS[d]), pl.ds(16 * d, 16)]
                thin_out[s, r, d] = (mine.astype(f32) + thin[s, r, 0, d].astype(f32)).astype(bf16)
                thin_move(s, r, d, 2).start()
        return carry

    lax.fori_loop(0, streams, step_four, 0)

    def step_five(s, carry):
        for r in range(2):
            for d in range(2):
                thin_move(s, r, d, 1).wait_recv()
                thin_move(s, r, d, 2).wait_recv()
            for d in range(2):
                rows = pl.ds(16 * d, 16)
                value = middle[s, r, at(r), rows].astype(f32) + thin[s, r, 2, d].astype(f32)
                value += thin[s, r, 1, 1 - d].astype(f32)
                total[s, pl.ds(32 * r + 16 * d, 16)] = value.astype(bf16)
        return carry

    lax.fori_loop(0, streams, step_five, 0)

    def swap(a):
        return remote(
            total.at[2 * a + 1 - ylo], out.at[a, ylo], swap_send.at[a], swap_recv.at[a], partner
        )

    def start_swap(a, carry):
        swap(a).start()
        return carry

    def finish_swap(a, carry):
        out[a, ylo] = total[2 * a + ylo]
        remote(
            total.at[2 * a], out.at[a, 1 - ylo], swap_send.at[a], swap_recv.at[a], partner
        ).wait_recv()
        swap(a).wait_send()
        return carry

    lax.fori_loop(0, streams // 2, start_swap, 0)

    def sent(s, carry):
        for r in range(2):
            for d in range(2):
                for kind in range(3):
                    wide_move(s, r, d, kind).wait_send()
                    thin_move(s, r, d, kind).wait_send()
        return carry

    lax.fori_loop(0, streams, sent, 0)
    lax.fori_loop(0, streams // 2, finish_swap, 0)


def weight_sum(grads, collective_id):
    arrays = grads.shape[0]
    n = arrays * 2
    return pl.pallas_call(
        weight_sum_kernel,
        out_shape=jax.ShapeDtypeStruct((arrays, 2, 64, PART), bf16),
        in_specs=[VMEM],
        out_specs=VMEM,
        scratch_shapes=[
            pltpu.VMEM((n, 2, 3, 2, 2, 32, PART), bf16),
            pltpu.VMEM((n, 2, 2, 2, 32, PART), bf16),
            pltpu.VMEM((n, 2, 4, 32, PART), bf16),
            pltpu.VMEM((n, 2, 3, 2, 16, PART), bf16),
            pltpu.VMEM((n, 2, 2, 16, PART), bf16),
            pltpu.VMEM((n, 64, PART), bf16),
            sems(arrays),
            sems(arrays),
            sems(n * 24),
            sems(n * 24),
        ],
        compiler_params=params(collective_id, 56),
    )(grads.reshape(arrays, 2, 4, 4, 64, PART))


def standardize(value):
    mean = jnp.mean(value, axis=-1, keepdims=True)
    centered = value - mean
    scale_inv = lax.rsqrt(jnp.mean(centered * centered, axis=-1, keepdims=True) + epsilon)
    return (centered * scale_inv, scale_inv)


def norm_back(grad_normed_out, normed, scale_inv, gain):
    scaled = grad_normed_out * gain
    mean_one = jnp.mean(scaled, axis=-1, keepdims=True)
    mean_two = jnp.mean(scaled * normed, axis=-1, keepdims=True)
    grad_value = scale_inv * (scaled - mean_one - normed * mean_two)
    grad_gain = jnp.sum(grad_normed_out * normed, axis=0)
    grad_shift = jnp.sum(grad_normed_out, axis=0)
    return (grad_value, grad_gain, grad_shift)


def visible(segment_ids, padding):
    seq_len = segment_ids.shape[1]
    position = jnp.arange(seq_len)
    causal = position[None, :] <= position[:, None]
    itself = position[None, :] == position[:, None]
    same = segment_ids[:, :, None] == segment_ids[:, None, :]
    live = (padding[:, None, :] == 1) | itself[None]
    return same & causal[None] & live


def score_block(query_heads, key_heads, allowed):
    scores = jnp.einsum(
        "rqhe,rkhe->rhqk", query_heads, key_heads, preferred_element_type=f32
    ) * HEAD ** (-0.5)
    return jnp.where(allowed[:, None], scores, masked_score)


def on_device(
    stream,
    code_ids,
    segment_ids,
    padding,
    codebook,
    norm1_gain,
    norm1_shift,
    w_qkv,
    w_out,
    norm2_gain,
    norm2_shift,
    w_up,
    w_down,
    cotangent,
):
    ylo, x, z, yhi, core = place()

    mine = jnp.stack(
        [
            jnp.concatenate(
                [
                    w_qkv.reshape(64, 3, 2, 256).transpose(2, 0, 1, 3).reshape(2, 64, 768),
                    w_out.reshape(64, 2, 256).transpose(1, 0, 2),
                ],
                axis=2,
            ),
            w_up.reshape(64, 2, PART).transpose(1, 0, 2),
            w_down.reshape(64, 2, PART).transpose(1, 0, 2),
        ]
    )
    weights = weight_gather(mine, 0).reshape(3, WIDTH, PART)
    qkv_full, out_full = weights[0, :, :768], weights[0, :, 768:]
    up_full, down_full = weights[1], weights[2]

    norms = jnp.stack([norm1_gain, norm1_shift, norm2_gain, norm2_shift]).astype(f32)
    masks = jnp.concatenate([segment_ids.reshape(4, 128), padding.reshape(4, 128)]).astype(f32)
    norms_all, masks_other = small_gather(jnp.pad(norms, ((0, 4), (0, 64))), masks, 1)
    norms_all = norms_all[:, :4, :64].transpose(1, 0, 2).reshape(4, WIDTH)
    gain_one, shift_one, gain_two, shift_two = norms_all
    both = jnp.where(ylo == 0, jnp.stack([masks, masks_other]), jnp.stack([masks_other, masks]))
    allowed = visible(both[:, :4].reshape(2, 512), both[:, 4:].reshape(2, 512))

    ids_half = lax.dynamic_slice_in_dim(code_ids[0], core * 256, 256, 0)
    stream_half = lax.dynamic_slice_in_dim(stream[0], core * 256, 256, 0)
    cot_half = lax.dynamic_slice_in_dim(cotangent[0], core * 256, 256, 0)
    inputs_half = stream_half.astype(f32) + jnp.take(codebook, ids_half, axis=0).astype(f32)
    normed_half, inv_half = standardize(inputs_half)
    attn_half = (normed_half * gain_one + shift_one).astype(bf16)

    def share_of(value):
        return lax.dynamic_slice_in_dim(value, yhi * SHARE, SHARE, 0)

    inputs_share, normed_one, inv_one = (share_of(v) for v in (inputs_half, normed_half, inv_half))
    cot_share = share_of(cot_half).astype(f32)

    rows = row_exchange(jnp.stack([attn_half, cot_half]).reshape(2, 2, SHARE, WIDTH), 2)
    attn_in, cot = rows[0].reshape(1024, WIDTH), rows[1].reshape(1024, WIDTH)

    projected = jnp.dot(attn_in, qkv_full, preferred_element_type=f32).astype(bf16)
    query_heads, key_heads, value_heads = (
        projected[:, 256 * t : 256 * t + 256].reshape(2, 512, 2, HEAD) for t in range(3)
    )
    scores = score_block(query_heads, key_heads, allowed)
    row_max = jnp.max(scores, axis=-1, keepdims=True)
    expd = jnp.exp(scores - row_max)
    row_sum = jnp.sum(expd, axis=-1, keepdims=True)
    log_total = row_max + jnp.log(row_sum)
    prob_low = (expd / row_sum).astype(bf16)
    attended = jnp.einsum("rhqk,rkhe->rqhe", prob_low, value_heads, preferred_element_type=f32)
    attended = attended.reshape(1024, 256).astype(bf16)
    partial_branch = jnp.einsum("sf,df->sd", attended, out_full, preferred_element_type=f32)
    middle = inputs_share + share_sum(partial_branch.astype(bf16), 3)
    normed_two, inv_two = standardize(middle)
    ffn_share = (normed_two * gain_two + shift_two).astype(bf16)
    ffn_in = share_gather(ffn_share, 4).reshape(1024, WIDTH)
    up_proj = jnp.dot(ffn_in, up_full, preferred_element_type=f32)
    hidden = jax.nn.gelu(up_proj, approximate=True).astype(bf16)
    partial_ffn = jnp.einsum("sf,df->sd", hidden, down_full, preferred_element_type=f32)
    layer_out = middle + share_sum(partial_ffn.astype(bf16), 5)

    grad_w_down = jnp.einsum("sd,sf->df", cot, hidden, preferred_element_type=f32).astype(bf16)
    grad_hidden = jnp.dot(cot, down_full, preferred_element_type=f32)
    _, gelu_pull = jax.vjp(lambda value: jax.nn.gelu(value, approximate=True), up_proj)
    grad_up = gelu_pull(grad_hidden)[0].astype(bf16)
    grad_w_up = jnp.einsum("sd,sf->df", ffn_in, grad_up, preferred_element_type=f32).astype(bf16)
    partial_ffn_in = jnp.einsum("sf,df->sd", grad_up, up_full, preferred_element_type=f32)
    grad_ffn_in = share_sum(partial_ffn_in.astype(bf16), 6)
    grad_norm_mid, grad_gain_two, grad_shift_two = norm_back(
        grad_ffn_in, normed_two, inv_two, gain_two
    )
    grad_middle = cot_share + grad_norm_mid
    grad_branch = share_gather(grad_middle.astype(bf16), 7).reshape(1024, WIDTH)
    grad_w_out = jnp.einsum("sd,sf->df", grad_branch, attended, preferred_element_type=f32)
    grad_attended = jnp.dot(grad_branch, out_full, preferred_element_type=f32).astype(bf16)
    grad_att_heads = grad_attended.reshape(2, 512, 2, HEAD)
    again_scores = score_block(query_heads, key_heads, allowed)
    probs = jnp.exp(again_scores - log_total)
    probs_low = probs.astype(bf16)
    grad_probs = jnp.einsum(
        "rqhe,rkhe->rhqk", grad_att_heads, value_heads, preferred_element_type=f32
    )
    inner = jnp.sum(grad_probs * probs, axis=-1, keepdims=True)
    grad_scores = (probs * (grad_probs - inner)).astype(bf16)
    grad_query = jnp.einsum(
        "rhqk,rkhe->rqhe", grad_scores, key_heads, preferred_element_type=f32
    ) * HEAD ** (-0.5)
    grad_key = jnp.einsum(
        "rhqk,rqhe->rkhe", grad_scores, query_heads, preferred_element_type=f32
    ) * HEAD ** (-0.5)
    grad_value = jnp.einsum(
        "rhqk,rqhe->rkhe", probs_low, grad_att_heads, preferred_element_type=f32
    )
    grad_projected = jnp.concatenate(
        [g.reshape(1024, 256) for g in (grad_query, grad_key, grad_value)], axis=1
    ).astype(bf16)
    grad_w_qkv = jnp.einsum("sd,sf->df", attn_in, grad_projected, preferred_element_type=f32)
    partial_attn_in = jnp.einsum("sf,df->sd", grad_projected, qkv_full, preferred_element_type=f32)
    grad_attn_in = share_sum(partial_attn_in.astype(bf16), 8)
    grad_norm_in, grad_gain_one, grad_shift_one = norm_back(
        grad_attn_in, normed_one, inv_one, gain_one
    )
    input_grad = grad_middle + grad_norm_in

    grads = jnp.stack(
        [
            jnp.concatenate([grad_w_qkv.astype(bf16), grad_w_out.astype(bf16)], axis=1),
            grad_w_up,
            grad_w_down,
        ]
    )
    summed = weight_sum(grads, 9).astype(f32)
    out_qkv = summed[0, :, :, :768].reshape(2, 64, 3, 256).transpose(1, 2, 0, 3).reshape(64, 3, 512)
    out_out = summed[0, :, :, 768:].transpose(1, 0, 2).reshape(64, 512)
    out_up = summed[1].transpose(1, 0, 2).reshape(64, WIDTH)
    out_down = summed[2].transpose(1, 0, 2).reshape(64, WIDTH)

    small = jnp.stack([grad_gain_one, grad_shift_one, grad_gain_two, grad_shift_two])
    small = jnp.pad(small.reshape(4, 32, 64).transpose(1, 0, 2), ((0, 0), (0, 4), (0, 64)))
    small = small_reduce(small, 10)[:4, :64]

    tokens = row_gather(jnp.stack([layer_out.astype(bf16), input_grad.astype(bf16)]), 11)
    tokens = tokens.reshape(2, 1, 512, WIDTH).astype(f32)
    return (
        tokens[0],
        tokens[1],
        small[0],
        small[1],
        out_qkv,
        out_out,
        small[2],
        small[3],
        out_up,
        out_down,
    )


def solution(mesh):
    in_specs = (
        P("dp", None, None),
        P("dp", None),
        P("dp", None),
        P("dp", None),
        P(),
        P("dp"),
        P("dp"),
        P("dp", None, "mp"),
        P("dp", "mp"),
        P("dp"),
        P("dp"),
        P("dp", "mp"),
        P("dp", "mp"),
        P("dp", None, None),
    )
    out_specs = (
        P("dp", None, None),
        P("dp", None, None),
        P("dp"),
        P("dp"),
        P("dp", None, "mp"),
        P("dp", "mp"),
        P("dp"),
        P("dp"),
        P("dp", "mp"),
        P("dp", "mp"),
    )
    return jax.shard_map(
        on_device, mesh=mesh, in_specs=in_specs, out_specs=out_specs, check_vma=False
    )
```

time: 1180 us -> 585 us (0.50)
  waiting for transfers between devices: 625 us -> 0 us
  Pallas kernels: 0 us -> 417 us
  blocking collectives: 151 us -> 0 us
  local copies, waits for them, and re-layouts: 188 us -> 53.8 us
  starting transfers between devices: 42.1 us -> 0 us
  matrix products: 97.7 us -> 74 us
  other arithmetic: 42.4 us -> 27.9 us
  between operations: 15.4 us -> 1.81 us
    pallas_call x0 -> x12, Pallas kernels: none -> 417 us  [the longest x4 116 us: share_sum(): pl.pallas_call(share_sum_kernel, out_shape=jax.ShapeDtypeStruct((SHARE, W...]
    all_gather x3 -> x0, waiting for transfers between devices: 252 us -> none  [the longest x2 252 us: gather_turned(): filled, at, done = (lax.all_gather(both, axis, axis=0, tiled=True), 0, [])]
    all_to_all x6 -> x0, waiting for transfers between devices: 197 us -> none  [the longest x4 173 us: sent_and_summed(): lax.all_to_all(pieces, axis, split_axis=0, concat_axis=0, tiled=True)]
    unnamed x6 -> x0, waiting for transfers between devices: 177 us -> none
    unnamed x1 -> x0, blocking collectives: 122 us -> none
    concatenate x4 -> x2, local copies, waits for them, and re-layouts: 102 us -> 6.48 us  [the longest x1 6.4 us: on_device(): jnp.concatenate([grad_w_qkv.astype(bf16), grad_w_out.astype(bf16)], axis=1)]
    all_to_all x6 -> x0, starting transfers between devices: 41.9 us -> none  [the longest x4 30.2 us: sent_and_summed(): lax.all_to_all(pieces, axis, split_axis=0, concat_axis=0, tiled=True)]
    dot_general x12, matrix products: 92.7 us -> 61.6 us  [the longest x1 8.26 us: on_device(): up_proj = jnp.dot(ffn_in, up_full, preferred_element_type=f32)]
  transfers between devices with their start and end apart: 11 -> 0, of which waited for: 8 -> 0; matrix products, arithmetic and copies ran while one was open for 22% -> 0% of each run, Pallas kernels for 0% -> 0%
where the time goes in v1:
time: 585 us; the launch traced here: 575 us
  Pallas kernels  417 us (71%)
  matrix products  74 us (13%)
  local copies, waits for them, and re-layouts  53.8 us (9%)
  other arithmetic  27.9 us (5%)
    pallas_call x4, Pallas kernels, share_sum(): pl.pallas_call(share_sum_kernel, out_shape=jax.ShapeDtypeStruct((SHARE, W...  116 us
    pallas_call x1, Pallas kernels, weight_sum(): pl.pallas_call(weight_sum_kernel, out_shape=jax.ShapeDtypeStruct((arrays,...  86.1 us
    pallas_call x1, Pallas kernels, weight_gather(): pl.pallas_call(weight_gather_kernel, out_shape=jax.ShapeDtypeStruct((arra...  75 us
    pallas_call x2, Pallas kernels, share_gather(): pl.pallas_call(share_gather_kernel, out_shape=jax.ShapeDtypeStruct((2, 2,...  58.9 us
    pallas_call x1, Pallas kernels, row_gather(): pl.pallas_call(row_gather_kernel, out_shape=jax.ShapeDtypeStruct((count,...  29.1 us
    pallas_call x1, Pallas kernels, row_exchange(): pl.pallas_call(functools.partial(row_exchange_kernel, count), out_shape=j...  27.1 us
    pallas_call x1, Pallas kernels, small_reduce(): pl.pallas_call(small_reduce_kernel, out_shape=jax.ShapeDtypeStruct((8, 12...  13.4 us
    pallas_call x1, Pallas kernels, small_gather(): pl.pallas_call(small_gather_kernel, out_shape=(jax.ShapeDtypeStruct((32,...  12.3 us

profile of v1, /device:TPU:16, one launch (start us, length us, event | category | flops | bytes accessed | tf_op | source)
XLA Modules:
  0.0 574.9 jit_solution(17642527597567233223)
XLA Ops:
  4.4 12.3 %shard_map.213 = (f32[32,8,128]{2,1,0:T(8,128)S(1)}, f32[8,128]{1,0:T(8,128)S(1)}) custom-call(f32[8,128]{1,0:T(8,128)S(1)} %fusion.52.own, f32[8,128]{1,0:T(8,128)S(1)} %add_convert_fusion.3.mask), custom_call_target="tpu_custom_call" | custom-call | tf_op jit(solution)/shard_map/pallas_call | solution.py:121
  19.9 1.5 or_and_fusion
  21.4 11.4 %gather_fusion = bf16[256,2048]{1,0:T(8,128)(2,1)} fusion(bf16[4096,2048]{1,0:T(8,128)(2,1)} %param.18, s32[1024]{0:T(1024)S(1)} %pad_clamp_fusion), kind=kCustom, calls=%fused_computation | custom fusion | bytes 2098176 | tf_op jit(solution)/shard_map/jit(_take)/gather | solution.py:791
  32.9 2.2 fusion.58
  35.1 1.7 multiply_reduce_fusion.1
  37.8 27.1 %shard_map.214 = bf16[2,2,2,2,128,2048]{5,4,3,2,1,0:T(8,128)(2,1)} custom-call(bf16[2,2,128,2048]{3,2,1,0:T(8,128)(2,1)S(1)} %pad_maximum_fusion.2.halves), custom_call_target="tpu_custom_call" | custom-call | tf_op jit(solution)/shard_map/pallas_call | solution.py:231
  64.9 5.4 fusion.61
  70.3 75.0 %shard_map.215 = bf16[3,2,4,4,64,1024]{5,4,3,2,1,0:T(8,128)(2,1)} custom-call(bf16[3,2,64,1024]{3,2,1,0:T(8,128)(2,1)S(1)} %pad_maximum_fusion.4.own), custom_call_target="tpu_custom_call" | custom-call | tf_op jit(solution)/shard_map/pallas_call | solution.py:518
  145.3 5.3 fusion.20
  153.0 2.0 reshape.391
  154.9 1.3 copy.77
  156.3 2.3 fusion.64
  159.2 1.4 copy-done.1
  160.6 1.7 fusion.29
  162.3 1.3 copy.71
  163.6 2.7 convolution_convert_fusion
  166.3 28.4 %shard_map.216 = f32[128,2048]{1,0:T(8,128)S(1)} custom-call(bf16[2,2,2,128,2048]{4,3,2,1,0:T(8,128)(2,1)S(1)} %bitcast.182), custom_call_target="tpu_custom_call" | custom-call | tf_op jit(solution)/shard_map/pallas_call | solution.py:332
  195.4 29.6 %shard_map.217 = bf16[2,2,2,128,2048]{4,3,2,1,0:T(8,128)(2,1)S(1)} custom-call(bf16[128,2048]{1,0:T(8,128)(2,1)S(1)} %add_convert_fusion.2.share), custom_call_target="tpu_custom_call" | custom-call | tf_op jit(solution)/shard_map/pallas_call | solution.py:271
  225.0 4.4 fusion.60
  229.7 4.5 fusion.65
  234.2 8.3 %fusion.6 = (bf16[1024,1024]{1,0:T(8,128)(2,1)S(1)}, f32[1024,1024]{1,0:T(8,128)}) fusion(f32[1024,1024]{1,0:T(8,128)S(1)} %fusion.65, bf16[1024,2048]{1,0:T(8,128)(2,1)S(1)} %bitcast.186, bf16[2048,1024]{1,0:T(8,128)(2,1)S(1)} %bitcast.208), kind=kOutput, calls=%fused_computation.10 | convolution fusion | flops 4315938816 | bytes 18874368 | tf_op jit(solution)/shard_map/dot_general | solution.py:821
  242.4 6.1 %convolution_convert_fusion.3 = bf16[2048,1024]{1,0:T(8,128)(2,1)} fusion(bf16[1024,2048]{1,0:T(8,128)(2,1)S(1)} %bitcast.187, bf16[1024,1024]{1,0:T(8,128)(2,1)S(1)} %get-tuple-element.54), kind=kOutput, calls=%fused_computation.22 | convolution fusion | flops 4297064448 | bytes 10485760 | tf_op jit(solution)/shard_map/sd,sf->df/dot_general | solution.py:830
  248.5 4.8 convolution_convert_fusion.4
  253.3 29.5 %shard_map.219 = f32[128,2048]{1,0:T(8,128)S(1)} custom-call(bf16[2,2,2,128,2048]{4,3,2,1,0:T(8,128)(2,1)S(1)} %bitcast.185), custom_call_target="tpu_custom_call" | custom-call | tf_op jit(solution)/shard_map/pallas_call | solution.py:332
  282.9 7.9 %convolution_convert_fusion.5 = bf16[1024,2048]{1,0:T(8,128)(2,1)S(1)} fusion(bf16[2048,1024]{1,0:T(8,128)(2,1)S(1)} %bitcast.207, f32[1024,1024]{1,0:T(8,128)} %get-tuple-element.55), kind=kOutput, calls=%fused_computation.24 | convolution fusion | flops 4306501632 | bytes 12582912 | tf_op jit(solution)/shard_map/sf,df->sd/dot_general | solution.py:823
  290.8 6.4 %convolution_convert_fusion.2 = bf16[2048,1024]{1,0:T(8,128)(2,1)} fusion(bf16[1024,2048]{1,0:T(8,128)(2,1)S(1)} %bitcast.203, f32[1024,1024]{1,0:T(8,128)S(1)} %copy-done.20), kind=kOutput, calls=%fused_computation.21 | convolution fusion | flops 4306501632 | bytes 12582912 | tf_op jit(solution)/shard_map/sd,sf->df/dot_general | solution.py:826
  297.2 29.3 %shard_map.218 = f32[128,2048]{1,0:T(8,128)S(1)} custom-call(bf16[2,2,2,128,2048]{4,3,2,1,0:T(8,128)(2,1)S(1)} %bitcast.184), custom_call_target="tpu_custom_call" | custom-call | tf_op jit(solution)/shard_map/pallas_call | solution.py:332
  326.6 1.2 multiply_reduce_fusion.2
  327.8 1.7 fusion.56
  329.7 29.3 %shard_map.220 = bf16[2,2,2,128,2048]{4,3,2,1,0:T(8,128)(2,1)S(1)} custom-call(bf16[128,2048]{1,0:T(8,128)(2,1)S(1)} %get-tuple-element.26.share), custom_call_target="tpu_custom_call" | custom-call | tf_op jit(solution)/shard_map/pallas_call | solution.py:271
  359.0 2.3 convolution_convert_fusion.7
  361.3 2.5 convolution_convert_fusion.8
  364.3 3.0 fusion.30
  367.4 1.3 copy.82
  368.8 3.2 multiply_reduce_fusion
  372.2 1.2 multiply_convert_fusion
  373.4 1.6 fusion.27
  375.9 1.3 copy.79
  377.5 7.0 %convolution_convert_fusion.1 = bf16[1024,2048]{1,0:T(8,128)(2,1)} fusion(bf16[1024,768]{1,0:T(8,128)(2,1)S(1)} %bitcast_dynamic-update-slice_fusion, bf16[3,2048,1024]{2,1,0:T(8,128)(2,1)} %bitcast.194), kind=kOutput, calls=%fused_computation.20 | convolution fusion | flops 3223322624 | bytes 8912896 | tf_op jit(solution)/shard_map/sf,df->sd/dot_general | solution.py:862
  384.5 3.8 convolution_convert_fusion.6
  388.4 2.3 pad_maximum_fusion.1
  390.7 6.4 %copy.83 = bf16[2048,1024]{1,0:T(8,128)(2,1)} copy(bf16[2048,1024]{0,1:T(8,128)(2,1)} %pad_maximum_fusion.1) | data formatting | bytes 8388608 | tf_op jit(solution)/shard_map/concatenate | solution.py:871
  397.1 9.6 %pad_maximum_fusion.grads = bf16[3,2,4,4,64,1024]{5,4,3,2,1,0:T(8,128)(2,1)} fusion(bf16[1,2,4,4,64,1024]{5,4,3,2,1,0:T(8,128)(2,1)} %bitcast.201, bf16[1,2,4,4,64,1024]{5,4,3,2,1,0:T(8,128)(2,1)} %bitcast.200, bf16[1,2,4,4,64,1024]{5,4,3,2,1,0:T(8,128)(2,1)} %bitcast.195), kind=kLoop, calls=%fused_computation.1 | loop fusion | flops 12582912 | bytes 25165824 | tf_op jit(solution)/shard_map/stack | solution.py:869
  406.7 86.1 %shard_map.224 = bf16[3,2,64,1024]{3,2,1,0:T(8,128)(2,1)} custom-call(bf16[3,2,4,4,64,1024]{5,4,3,2,1,0:T(8,128)(2,1)} %pad_maximum_fusion.grads), custom_call_target="tpu_custom_call" | custom-call | tf_op jit(solution)/shard_map/pallas_call | solution.py:690
  492.9 28.4 %shard_map.221 = f32[128,2048]{1,0:T(8,128)S(1)} custom-call(bf16[2,2,2,128,2048]{4,3,2,1,0:T(8,128)(2,1)S(1)} %bitcast.183), custom_call_target="tpu_custom_call" | custom-call | tf_op jit(solution)/shard_map/pallas_call | solution.py:332
  522.7 13.4 %shard_map.223 = f32[8,128]{1,0:T(8,128)S(1)} custom-call(f32[32,8,128]{2,1,0:T(8,128)S(1)} %pad.12.pieces), custom_call_target="tpu_custom_call" | custom-call | tf_op jit(solution)/shard_map/pallas_call | solution.py:177
  540.9 29.1 %shard_map.222 = bf16[2,2,2,128,2048]{4,3,2,1,0:T(8,128)(2,1)S(1)} custom-call(bf16[2,128,2048]{2,1,0:T(8,128)(2,1)S(1)} %pad_maximum_fusion.3.share), custom_call_target="tpu_custom_call" | custom-call | tf_op jit(solution)/shard_map/pallas_call | solution.py:375
  570.0 4.5 fusion.62
  (114 shorter events, 20.1 us)
Async XLA Ops:
  21.4 11.4 %copy-start.18 = (bf16[1,512,2048]{2,1,0:T(8,128)(2,1)S(1)}, bf16[1,512,2048]{2,1,0:T(8,128)(2,1)}, u32[]{:S(2)}) copy-start(bf16[1,512,2048]{2,1,0:T(8,128)(2,1)} %param.27) | copy-start | bytes 6291460
  32.9 3.9 copy-start.3
  32.9 3.9 copy-start.15
  70.3 75.0 %copy-start.8 = (bf16[1,2,2,2,128,2048]{5,4,3,2,1,0:T(8,128)(2,1)}, bf16[1,2,2,2,128,2048]{5,4,3,2,1,0:T(8,128)(2,1)S(1)}, u32[]{:S(2)}) copy-start(bf16[1,2,2,2,128,2048]{5,4,3,2,1,0:T(8,128)(2,1)S(1)} %get-tuple-element.39) | copy-start | bytes 12582916
  156.2 2.9 copy-start.6
  156.2 4.3 copy-start.13
  158.6 2.0 copy-start.1
  163.6 2.7 copy-start.11
  225.0 4.7 copy-start.10
  282.9 8.0 %copy-start.20 = (f32[1024,1024]{1,0:T(8,128)S(1)}, f32[1024,1024]{1,0:T(8,128)}, u32[]{:S(2)}) copy-start(f32[1024,1024]{1,0:T(8,128)} %get-tuple-element.55) | copy-start | bytes 12582916
  327.8 31.2 %copy-start.12 = (bf16[2,512,2,128]{3,2,1,0:T(2,128)(2,1)S(1)}, bf16[2,512,2,128]{3,2,1,0:T(2,128)(2,1)}, u32[]{:S(2)}) copy-start(bf16[2,512,2,128]{3,2,1,0:T(2,128)(2,1)} %copy-done.11) | copy-start | bytes 1572868
  363.8 5.0 copy-start.14
  368.7 3.5 copy-start.2
  372.2 1.2 copy-start.7
  375.0 2.4 copy-start.17
  377.5 7.1 %copy-start.9 = (bf16[1,2,2,2,128,2048]{5,4,3,2,1,0:T(8,128)(2,1)S(1)}, bf16[1,2,2,2,128,2048]{5,4,3,2,1,0:T(8,128)(2,1)}, u32[]{:S(2)}) copy-start(bf16[1,2,2,2,128,2048]{5,4,3,2,1,0:T(8,128)(2,1)} %copy-done.8) | copy-start | bytes 12582916
  384.5 3.8 copy-start.19
  406.7 86.1 %copy-start = (bf16[1024,2048]{1,0:T(8,128)(2,1)S(1)}, bf16[1024,2048]{1,0:T(8,128)(2,1)}, u32[]{:S(2)}) copy-start(bf16[1024,2048]{1,0:T(8,128)(2,1)} %convolution_convert_fusion.1) | copy-start | bytes 12582916
  492.8 28.4 %copy-start.4 = (f32[256,2048]{1,0:T(8,128)S(1)}, f32[256,2048]{1,0:T(8,128)}, u32[]{:S(2)}) copy-start(f32[256,2048]{1,0:T(8,128)} %get-tuple-element.31) | copy-start | bytes 6291460
  521.3 1.0 copy-start.16
  521.3 15.3 %copy-start.5 = (bf16[3,2,64,1024]{3,2,1,0:T(8,128)(2,1)S(1)}, bf16[3,2,64,1024]{3,2,1,0:T(8,128)(2,1)}, u32[]{:S(2)}) copy-start(bf16[3,2,64,1024]{3,2,1,0:T(8,128)(2,1)} %shard_map.224) | copy-start | bytes 2359300

commit v2 on v0

v2 whole, which is shorter than its diff:
```python
import functools

import jax
import jax.numpy as jnp
from jax import lax
from jax.experimental import pallas as pl
from jax.experimental.pallas import tpu as pltpu
from jax.sharding import PartitionSpec as P

HEAD = 128
WIDTH = 2048
SHARE = 128
PART = 1024
MESH = pl.DeviceIdType.MESH
ANY = pl.BlockSpec(memory_space=pl.ANY)
VMEM = pl.BlockSpec(memory_space=pltpu.VMEM)
masked_score = -1000000000.0
epsilon = 1e-05
f32 = jnp.float32
bf16 = jnp.bfloat16


def place():
    dp, mp = lax.axis_index("dp"), lax.axis_index("mp")
    return lax.div(dp, 16), lax.rem(lax.div(dp, 4), 4), lax.rem(dp, 4), lax.div(mp, 2), lax.rem(mp, 2)


def ring(position, step):
    return lax.rem(position + step + 4, 4)


def xz_neighbour(axis, step):
    ylo, x, z, yhi, core = place()
    if axis == 0:
        x = ring(x, step)
    else:
        z = ring(z, step)
    return (ylo * 16 + x * 4 + z, yhi * 2 + core)


def y_peer(step):
    ylo, x, z, yhi, core = place()
    y = ring(yhi * 2 + ylo, step)
    return (lax.rem(y, 2) * 16 + x * 4 + z, lax.div(y, 2) * 2 + core)


def lo_partner():
    ylo, x, z, yhi, core = place()
    return ((1 - ylo) * 16 + x * 4 + z, yhi * 2 + core)


def core_partner():
    ylo, x, z, yhi, core = place()
    return (ylo * 16 + x * 4 + z, yhi * 2 + 1 - core)


def greet(peers):
    barrier = pltpu.get_barrier_semaphore()
    for peer in peers:
        pl.semaphore_signal(barrier, inc=1, device_id=peer, device_id_type=MESH)
    pl.semaphore_wait(barrier, len(peers))


def remote(src, dst, send_sem, recv_sem, peer):
    return pltpu.make_async_remote_copy(
        src_ref=src,
        dst_ref=dst,
        send_sem=send_sem,
        recv_sem=recv_sem,
        device_id=peer,
        device_id_type=MESH,
    )


def sems(*shape):
    return pltpu.SemaphoreType.DMA(shape)


def params(collective_id, mib=48):
    return pltpu.CompilerParams(
        collective_id=collective_id, has_side_effects=True, vmem_limit_bytes=mib << 20
    )


PEERS = {
    "core": core_partner,
    "x+": lambda: xz_neighbour(0, 1),
    "x-": lambda: xz_neighbour(0, -1),
    "z+": lambda: xz_neighbour(1, 1),
    "z-": lambda: xz_neighbour(1, -1),
    "y1": lambda: y_peer(1),
    "y2": lambda: y_peer(2),
    "y3": lambda: y_peer(3),
}


def fused_kernel(jobs, schedule, *refs):
    taken = 0

    def take(count):
        nonlocal taken
        taken += count
        return refs[taken - count : taken]

    ins = [take(len(job["ins"])) for job in jobs]
    outs = [take(len(job["outs"])) for job in jobs]
    scratch = [take(len(job["scratch"])) for job in jobs]
    greet([PEERS[name]() for name in sorted({name for job in jobs for name in job["peers"]})])
    runs = [job["steps"](*i, *o, *s) for job, i, o, s in zip(jobs, ins, outs, scratch)]
    for which in schedule:
        next(runs[int(which)], None)
    for run in runs:
        for _ in run:
            pass


def fused(jobs, schedule, collective_id, mib=48):
    results = pl.pallas_call(
        functools.partial(fused_kernel, jobs, schedule),
        out_shape=[shape for job in jobs for shape, _ in job["outs"]],
        in_specs=[spec for job in jobs for _, spec in job["ins"]],
        out_specs=[spec for job in jobs for _, spec in job["outs"]],
        scratch_shapes=[one for job in jobs for one in job["scratch"]],
        compiler_params=params(collective_id, mib),
    )(*[array for job in jobs for array, _ in job["ins"]])
    return results


def shaped(dtype, *shape):
    return jax.ShapeDtypeStruct(shape, dtype)


def small_gather_kernel(own, mask, everyone, mask_out, send, recv, mask_send, mask_recv):
    dp, mp = lax.axis_index("dp"), lax.axis_index("mp")
    barrier = pltpu.get_barrier_semaphore()

    def greet_one(k, carry):
        pl.semaphore_signal(
            barrier, inc=1, device_id=(lax.rem(dp + k, 32), mp), device_id_type=MESH
        )
        return carry

    lax.fori_loop(1, 32, greet_one, 0)
    pl.semaphore_wait(barrier, 31)

    def move(k):
        peer = lax.rem(dp + k, 32)
        return remote(own, everyone.at[dp], send.at[k], recv.at[dp], (peer, mp))

    def start(k, carry):
        move(k).start()
        return carry

    def finish(k, carry):
        source = lax.rem(dp + k, 32)
        move(k).wait_send()
        remote(own, everyone.at[source], send.at[k], recv.at[source], (source, mp)).wait_recv()
        return carry

    swap = remote(mask, mask_out, mask_send, mask_recv, lo_partner())
    swap.start()
    lax.fori_loop(1, 32, start, 0)
    everyone[dp] = own[...]
    lax.fori_loop(1, 32, finish, 0)
    swap.wait()


def small_gather(own, mask, collective_id):
    return pl.pallas_call(
        small_gather_kernel,
        out_shape=(
            jax.ShapeDtypeStruct((32, 8, 128), f32),
            jax.ShapeDtypeStruct((8, 128), f32),
        ),
        in_specs=[VMEM, VMEM],
        out_specs=(VMEM, VMEM),
        scratch_shapes=[sems(32), sems(32), pltpu.SemaphoreType.DMA, pltpu.SemaphoreType.DMA],
        compiler_params=params(collective_id, 8),
    )(own, mask)


def small_reduce_kernel(pieces, out, arrived, summed, more, send, recv, send_two, recv_two):
    dp, mp = lax.axis_index("dp"), lax.axis_index("mp")
    barrier = pltpu.get_barrier_semaphore()

    def greet_one(k, carry):
        pl.semaphore_signal(
            barrier, inc=1, device_id=(lax.rem(dp + k, 32), mp), device_id_type=MESH
        )
        return carry

    lax.fori_loop(1, 32, greet_one, 0)
    for k in (1, 2, 3):
        pl.semaphore_signal(
            barrier, inc=1, device_id=(dp, lax.rem(mp + k, 4)), device_id_type=MESH
        )
    pl.semaphore_wait(barrier, 34)

    def move(k):
        peer = lax.rem(dp + k, 32)
        return remote(pieces.at[peer], arrived.at[k], send.at[k], recv.at[k], (peer, mp))

    def start(k, carry):
        move(k).start()
        return carry

    def finish(k, total):
        move(k).wait()
        return total + arrived[k]

    lax.fori_loop(1, 32, start, 0)
    summed[...] = lax.fori_loop(1, 32, finish, pieces[dp])
    copies = [
        remote(summed, more.at[k - 1], send_two.at[k], recv_two.at[k], (dp, lax.rem(mp + k, 4)))
        for k in (1, 2, 3)
    ]
    for copy in copies:
        copy.start()
    for copy in copies:
        copy.wait()
    out[...] = summed[...] + more[0] + more[1] + more[2]


def small_reduce(pieces, collective_id):
    return pl.pallas_call(
        small_reduce_kernel,
        out_shape=jax.ShapeDtypeStruct((8, 128), f32),
        in_specs=[VMEM],
        out_specs=VMEM,
        scratch_shapes=[
            pltpu.VMEM((32, 8, 128), f32),
            pltpu.VMEM((8, 128), f32),
            pltpu.VMEM((3, 8, 128), f32),
            sems(32),
            sems(32),
            sems(4),
            sems(4),
        ],
        compiler_params=params(collective_id, 8),
    )(pieces)


def row_exchange(halves):
    count = halves.shape[0]

    def steps(halves, full, local_sem, send, recv):
        ylo, x, z, yhi, core = place()
        up, down, other = y_peer(1), y_peer(3), core_partner()
        first = []
        for n in range(count):
            for u, peer in ((0, up), (1, down)):
                here = full.at[n, ylo, core, u]
                first.append(remote(halves.at[n, u], here, send.at[n, u], recv.at[n, u], peer))
        for n in range(count):
            here = full.at[n, ylo, core]
            first.append(remote(halves.at[n], here, send.at[n, 2], recv.at[n, 2], other))
        for copy in first:
            copy.start()
        local = [
            pltpu.make_async_copy(halves.at[n], full.at[n, ylo, core], local_sem.at[n])
            for n in range(count)
        ]
        for copy in local:
            copy.start()
        yield
        second = []
        for n in range(count):
            for u in range(2):
                here = full.at[n, 1 - ylo, core, u]
                remote(halves.at[n, u], here, send.at[n, u], recv.at[n, u], up).wait_recv()
                copy = remote(here, here, send.at[n, 3 + u], recv.at[n, 3 + u], other)
                copy.start()
                second.append(copy)
        yield
        for n in range(count):
            here = full.at[n, ylo, 1 - core]
            remote(halves.at[n], here, send.at[n, 2], recv.at[n, 2], other).wait_recv()
            for u in range(2):
                here = full.at[n, 1 - ylo, 1 - core, u]
                remote(here, here, send.at[n, 3 + u], recv.at[n, 3 + u], other).wait_recv()
        for copy in first + second:
            copy.wait_send()
        for copy in local:
            copy.wait()

    return {
        "ins": [(halves, ANY)],
        "outs": [(shaped(bf16, count, 2, 2, 2, SHARE, WIDTH), ANY)],
        "scratch": [sems(count), sems(count, 5), sems(count, 5)],
        "peers": ["y1", "y3", "core"],
        "steps": steps,
    }


def share_gather(share):
    def steps(share, full, local_sem, send, recv):
        ylo, x, z, yhi, core = place()
        y = yhi * 2 + ylo
        other = core_partner()
        mine = full.at[ylo, core, yhi]
        local = pltpu.make_async_copy(share, mine, local_sem)
        first = [
            remote(share, mine, send.at[k], recv.at[k], y_peer(k) if k else other)
            for k in (2, 1, 3, 0)
        ]
        for copy in first:
            copy.start()
        local.start()
        yield
        second = []
        for k in (1, 3, 2):
            source = ring(y, -k)
            here = full.at[lax.rem(source, 2), core, lax.div(source, 2)]
            remote(share, here, send.at[k], recv.at[k], y_peer(4 - k)).wait_recv()
            copy = remote(here, here, send.at[3 + k], recv.at[3 + k], other)
            copy.start()
            second.append(copy)
        yield
        remote(share, full.at[ylo, 1 - core, yhi], send.at[0], recv.at[0], other).wait_recv()
        for k in (1, 3, 2):
            source = ring(y, -k)
            here = full.at[lax.rem(source, 2), 1 - core, lax.div(source, 2)]
            remote(here, here, send.at[3 + k], recv.at[3 + k], other).wait_recv()
        for copy in first + second:
            copy.wait_send()
        local.wait()

    return {
        "ins": [(share, ANY)],
        "outs": [(shaped(bf16, 2, 2, 2, SHARE, WIDTH), ANY)],
        "scratch": [pltpu.SemaphoreType.DMA, sems(7), sems(7)],
        "peers": ["y1", "y2", "y3", "core"],
        "steps": steps,
    }


def add_rows(count, one):
    def body(i, carry):
        one(pl.ds(pl.multiple_of(i * 16, 16), 16))
        return carry

    lax.fori_loop(0, count // 16, body, 0)


def share_sum(partial):
    def steps(partial, out, from_core, turned, arrived, send, recv, send_two, recv_two):
        ylo, x, z, yhi, core = place()
        y = yhi * 2 + ylo
        other = core_partner()

        def block(k, half):
            target = ring(y, k)
            return partial.at[lax.rem(target, 2), half, lax.div(target, 2)]

        first = {}
        for k in (2, 1, 3, 0):
            first[k] = remote(block(k, 1 - core), from_core.at[k], send.at[k], recv.at[k], other)
            first[k].start()
        yield
        second = {}
        for k in (2, 1, 3):
            first[k].wait_recv()
            mine = block(k, core)

            def add(rows):
                value = mine[rows].astype(f32) + from_core[k, rows].astype(f32)
                turned[k, rows] = value.astype(bf16)

            add_rows(SHARE, add)
            second[k] = remote(turned.at[k], arrived.at[k], send_two.at[k], recv_two.at[k], y_peer(k))
            second[k].start()
        yield
        first[0].wait_recv()
        for k in (1, 3, 2):
            second[k].wait_recv()
        mine_own = block(0, core)

        def total(rows):
            value = mine_own[rows].astype(f32) + from_core[0, rows].astype(f32)
            for k in (1, 2, 3):
                value += arrived[k, rows].astype(f32)
            out[rows] = value

        add_rows(SHARE, total)
        for k in range(4):
            first[k].wait_send()
        for k in (1, 2, 3):
            second[k].wait_send()

    return {
        "ins": [(partial.reshape(2, 2, 2, SHARE, WIDTH), VMEM)],
        "outs": [(shaped(f32, SHARE, WIDTH), VMEM)],
        "scratch": [pltpu.VMEM((4, SHARE, WIDTH), bf16)] * 3 + [sems(4)] * 4,
        "peers": ["y1", "y2", "y3", "core"],
        "steps": steps,
    }


def row_gather(share):
    count = share.shape[0]

    def steps(share, full, local_sem, send, recv):
        ylo, x, z, yhi, core = place()
        across, other = y_peer(2), core_partner()
        mine = full.at[:, core, yhi]
        far = full.at[:, core, 1 - yhi]
        local = pltpu.make_async_copy(share, mine, local_sem)
        one = remote(share, mine, send.at[0], recv.at[0], across)
        two = remote(share, mine, send.at[1], recv.at[1], other)
        one.start()
        two.start()
        local.start()
        yield
        remote(share, far, send.at[0], recv.at[0], across).wait_recv()
        three = remote(far, far, send.at[2], recv.at[2], other)
        three.start()
        yield
        remote(share, full.at[:, 1 - core, yhi], send.at[1], recv.at[1], other).wait_recv()
        last = full.at[:, 1 - core, 1 - yhi]
        remote(last, last, send.at[2], recv.at[2], other).wait_recv()
        for copy in (one, two, three):
            copy.wait_send()
        local.wait()

    return {
        "ins": [(share, ANY)],
        "outs": [(shaped(bf16, count, 2, 2, SHARE, WIDTH), ANY)],
        "scratch": [pltpu.SemaphoreType.DMA, sems(3), sems(3)],
        "peers": ["y2", "core"],
        "steps": steps,
    }


SIGNS = (1, -1)
XZ = ["x+", "x-", "z+", "z-"]


def xz_near():
    return [[xz_neighbour(axis, d) for d in SIGNS] for axis in (0, 1)]


def weight_gather(own):
    def steps(own, full, local_sem, swap_send, swap_recv, send, recv):
        ylo, x, z, yhi, core = place()
        near = xz_near()
        partner = lo_partner()
        offsets = (0, -1, 1, 2)

        def move(src, dst, s, r, stage, d, axis):
            n = ((s * 2 + r) * 8 + stage) * 2 + d
            return remote(src, dst, send.at[n], recv.at[n], near[axis][d])

        def block(s, r, one, two, rows):
            yl = ylo if s == 0 else 1 - ylo
            if r == 0:
                return full.at[yl, ring(x, one), ring(z, two), rows]
            return full.at[yl, ring(x, two), ring(z, one), rows]

        def rows_of(r, d=None):
            return pl.ds(32 * r, 32) if d is None else pl.ds(32 * r + 16 * d, 16)

        local = pltpu.make_async_copy(own.at[ylo], full.at[ylo, x, z], local_sem)
        swap = remote(own.at[1 - ylo], full.at[ylo, x, z], swap_send, swap_recv, partner)
        swap.start()
        sent = []

        def go(*args):
            copy = move(*args)
            copy.start()
            sent.append(copy)

        def begin(s, source):
            for r in range(2):
                for d in range(2):
                    src = source.at[rows_of(r)]
                    go(src, block(s, r, 0, 0, rows_of(r)), s, r, 0, d, r)
            for r in range(2):
                for d in range(2):
                    src = source.at[rows_of(r)]
                    go(src, block(s, r, 0, 0, rows_of(r)), s, r, 2, d, 1 - r)

        begin(0, own.at[ylo])
        local.start()
        yield
        remote(own.at[1 - ylo], full.at[1 - ylo, x, z], swap_send, swap_recv, partner).wait_recv()
        begin(1, full.at[1 - ylo, x, z])
        yield
        for s in range(2):
            for r in range(2):
                for d in range(2):
                    came = block(s, r, -SIGNS[d], 0, rows_of(r))
                    move(came, came, s, r, 0, d, r).wait_recv()
                    piece = block(s, r, -SIGNS[d], 0, rows_of(r, d))
                    go(piece, piece, s, r, 1, d, r)
                for part in (1, 2):
                    for d in range(2):
                        mine = block(s, r, offsets[part], 0, rows_of(r))
                        go(mine, mine, s, r, 2 + part, d, 1 - r)
            yield
        for s in range(2):
            for r in range(2):
                for d in range(2):
                    piece = block(s, r, 2, 0, rows_of(r, d))
                    move(piece, piece, s, r, 1, d, r).wait_recv()
                for d in range(2):
                    mine = block(s, r, 2, 0, rows_of(r))
                    go(mine, mine, s, r, 5, d, 1 - r)
            yield
        for part in (0, 2, 1, 3):
            d = part // 2
            for s in range(2):
                for r in range(2):
                    came = block(s, r, offsets[part], -SIGNS[d], rows_of(r))
                    move(came, came, s, r, 2 + part, d, 1 - r).wait_recv()
                    go(came, came, s, r, 6 + part % 2, d, 1 - r)
            yield
        for s in range(2):
            for r in range(2):
                for part in range(4):
                    d = 1 - part // 2
                    came = block(s, r, offsets[part], -SIGNS[d], rows_of(r))
                    move(came, came, s, r, 2 + part, d, 1 - r).wait_recv()
                for part in range(4):
                    d = part // 2
                    came = block(s, r, offsets[part], 2, rows_of(r))
                    move(came, came, s, r, 6 + part % 2, d, 1 - r).wait_recv()
        for copy in sent:
            copy.wait_send()
        swap.wait_send()
        local.wait()

    return {
        "ins": [(own, ANY)],
        "outs": [(shaped(bf16, 2, 4, 4, 64, PART), ANY)],
        "scratch": [pltpu.SemaphoreType.DMA] * 3 + [sems(64), sems(64)],
        "peers": XZ + ["y1", "y3"],
        "steps": steps,
    }


def weight_sum(grads):
    def steps(grads, out, wide, wide_out, middle, thin, thin_out, total, swap_send, swap_recv, send, recv):
        ylo, x, z, yhi, core = place()
        near = xz_near()
        partner = lo_partner()

        def move(src, dst, s, r, stage, d, axis):
            n = ((s * 2 + r) * 6 + stage) * 2 + d
            return remote(src, dst, send.at[n], recv.at[n], near[axis][d])

        def line(s, r, step, part):
            if r == 0:
                return grads.at[s, part, ring(z, step), pl.ds(0, 32)]
            return grads.at[s, ring(x, step), part, pl.ds(32, 32)]

        def at(r):
            return x if r == 0 else z

        def wide_move(s, r, d, kind):
            if kind == 0:
                src = line(s, r, 2, pl.ds(2 * d, 2))
            elif kind == 1:
                src = line(s, r, SIGNS[d], pl.ds(2 - 2 * d, 2))
            else:
                src = wide_out.at[s, r, d]
            return move(src, wide.at[s, r, kind, d], s, r, kind, d, 1 - r)

        def thin_move(s, r, d, kind):
            if kind == 0:
                src = middle.at[s, r, ring(at(r), 2), pl.ds(16 * d, 16)]
            elif kind == 1:
                src = middle.at[s, r, ring(at(r), SIGNS[d]), pl.ds(16 - 16 * d, 16)]
            else:
                src = thin_out.at[s, r, d]
            return move(src, thin.at[s, r, kind, d], s, r, 3 + kind, d, r)

        for s in range(2):
            for kind in range(2):
                for r in range(2):
                    for d in range(2):
                        wide_move(s, r, d, kind).start()
        yield

        def step_two(s, carry):
            for r in range(2):
                for d in range(2):
                    wide_move(s, r, d, 0).wait_recv()
                    for p in range(2):
                        mine = line(s, r, SIGNS[d], 2 * d + p)

                        def one(rows):
                            value = mine[rows].astype(f32) + wide[s, r, 0, d, p, rows].astype(f32)
                            wide_out[s, r, d, p, rows] = value.astype(bf16)

                        add_rows(32, one)
                    wide_move(s, r, d, 2).start()
            return carry

        lax.fori_loop(0, 2, step_two, 0)
        yield

        def step_three(s, carry):
            for r in range(2):
                for d in range(2):
                    wide_move(s, r, d, 1).wait_recv()
                    wide_move(s, r, d, 2).wait_recv()
                for p in range(4):
                    mine = line(s, r, 0, p)
                    d = p // 2

                    def one(rows):
                        value = mine[rows].astype(f32) + wide[s, r, 2, d, p % 2, rows].astype(f32)
                        value += wide[s, r, 1, 1 - d, p % 2, rows].astype(f32)
                        middle[s, r, p, rows] = value.astype(bf16)

                    add_rows(32, one)
                for kind in range(2):
                    for d in range(2):
                        thin_move(s, r, d, kind).start()
            return carry

        lax.fori_loop(0, 2, step_three, 0)
        yield

        def step_four(s, carry):
            for r in range(2):
                for d in range(2):
                    thin_move(s, r, d, 0).wait_recv()
                    mine = middle[s, r, ring(at(r), SIGNS[d]), pl.ds(16 * d, 16)]
                    value = mine.astype(f32) + thin[s, r, 0, d].astype(f32)
                    thin_out[s, r, d] = value.astype(bf16)
                    thin_move(s, r, d, 2).start()
            return carry

        lax.fori_loop(0, 2, step_four, 0)
        yield

        def step_five(s, carry):
            for r in range(2):
                for d in range(2):
                    thin_move(s, r, d, 1).wait_recv()
                    thin_move(s, r, d, 2).wait_recv()
                for d in range(2):
                    rows = pl.ds(16 * d, 16)
                    value = middle[s, r, at(r), rows].astype(f32) + thin[s, r, 2, d].astype(f32)
                    value += thin[s, r, 1, 1 - d].astype(f32)
                    total[s, pl.ds(32 * r + 16 * d, 16)] = value.astype(bf16)
            return carry

        lax.fori_loop(0, 2, step_five, 0)
        swap = remote(total.at[1 - ylo], out.at[ylo], swap_send, swap_recv, partner)
        swap.start()
        out[ylo] = total[ylo]
        yield
        for s in range(2):
            for r in range(2):
                for d in range(2):
                    for kind in range(3):
                        wide_move(s, r, d, kind).wait_send()
                        thin_move(s, r, d, kind).wait_send()
        remote(total.at[0], out.at[1 - ylo], swap_send, swap_recv, partner).wait_recv()
        swap.wait_send()

    return {
        "ins": [(grads.reshape(2, 4, 4, 64, PART), VMEM)],
        "outs": [(shaped(bf16, 2, 64, PART), VMEM)],
        "scratch": [
            pltpu.VMEM((2, 2, 3, 2, 2, 32, PART), bf16),
            pltpu.VMEM((2, 2, 2, 2, 32, PART), bf16),
            pltpu.VMEM((2, 2, 4, 32, PART), bf16),
            pltpu.VMEM((2, 2, 3, 2, 16, PART), bf16),
            pltpu.VMEM((2, 2, 2, 16, PART), bf16),
            pltpu.VMEM((2, 64, PART), bf16),
            pltpu.SemaphoreType.DMA,
            pltpu.SemaphoreType.DMA,
            sems(48),
            sems(48),
        ],
        "peers": XZ + ["y1", "y3"],
        "steps": steps,
    }


def standardize(value):
    mean = jnp.mean(value, axis=-1, keepdims=True)
    centered = value - mean
    scale_inv = lax.rsqrt(jnp.mean(centered * centered, axis=-1, keepdims=True) + epsilon)
    return (centered * scale_inv, scale_inv)


def norm_back(grad_normed_out, normed, scale_inv, gain):
    scaled = grad_normed_out * gain
    mean_one = jnp.mean(scaled, axis=-1, keepdims=True)
    mean_two = jnp.mean(scaled * normed, axis=-1, keepdims=True)
    grad_value = scale_inv * (scaled - mean_one - normed * mean_two)
    grad_gain = jnp.sum(grad_normed_out * normed, axis=0)
    grad_shift = jnp.sum(grad_normed_out, axis=0)
    return (grad_value, grad_gain, grad_shift)


def visible(segment_ids, padding):
    seq_len = segment_ids.shape[1]
    position = jnp.arange(seq_len)
    causal = position[None, :] <= position[:, None]
    itself = position[None, :] == position[:, None]
    same = segment_ids[:, :, None] == segment_ids[:, None, :]
    live = (padding[:, None, :] == 1) | itself[None]
    return same & causal[None] & live


def score_block(query_heads, key_heads, allowed):
    scores = jnp.einsum(
        "rqhe,rkhe->rhqk", query_heads, key_heads, preferred_element_type=f32
    ) * HEAD ** (-0.5)
    return jnp.where(allowed[:, None], scores, masked_score)


def on_device(
    stream,
    code_ids,
    segment_ids,
    padding,
    codebook,
    norm1_gain,
    norm1_shift,
    w_qkv,
    w_out,
    norm2_gain,
    norm2_shift,
    w_up,
    w_down,
    cotangent,
):
    ylo, x, z, yhi, core = place()

    own_attn = jnp.concatenate(
        [
            w_qkv.reshape(64, 3, 2, 256).transpose(2, 0, 1, 3).reshape(2, 64, 768),
            w_out.reshape(64, 2, 256).transpose(1, 0, 2),
        ],
        axis=2,
    )
    own_up = w_up.reshape(64, 2, PART).transpose(1, 0, 2)
    own_down = w_down.reshape(64, 2, PART).transpose(1, 0, 2)

    norms = jnp.stack([norm1_gain, norm1_shift, norm2_gain, norm2_shift]).astype(f32)
    masks = jnp.concatenate([segment_ids.reshape(4, 128), padding.reshape(4, 128)]).astype(f32)
    norms_all, masks_other = small_gather(jnp.pad(norms, ((0, 4), (0, 64))), masks, 1)
    norms_all = norms_all[:, :4, :64].transpose(1, 0, 2).reshape(4, WIDTH)
    gain_one, shift_one, gain_two, shift_two = norms_all
    both = jnp.where(ylo == 0, jnp.stack([masks, masks_other]), jnp.stack([masks_other, masks]))
    allowed = visible(both[:, :4].reshape(2, 512), both[:, 4:].reshape(2, 512))

    ids_half = lax.dynamic_slice_in_dim(code_ids[0], core * 256, 256, 0)
    stream_half = lax.dynamic_slice_in_dim(stream[0], core * 256, 256, 0)
    cot_half = lax.dynamic_slice_in_dim(cotangent[0], core * 256, 256, 0)
    inputs_half = stream_half.astype(f32) + jnp.take(codebook, ids_half, axis=0).astype(f32)
    normed_half, inv_half = standardize(inputs_half)
    attn_half = (normed_half * gain_one + shift_one).astype(bf16)

    def share_of(value):
        return lax.dynamic_slice_in_dim(value, yhi * SHARE, SHARE, 0)

    inputs_share, normed_one, inv_one = (share_of(v) for v in (inputs_half, normed_half, inv_half))
    cot_share = share_of(cot_half).astype(f32)

    halves = jnp.stack([attn_half, cot_half]).reshape(2, 2, SHARE, WIDTH)
    rows, attn_full = fused([row_exchange(halves), weight_gather(own_attn)], "0111101111", 2)
    attn_full = attn_full.reshape(WIDTH, PART)
    qkv_full, out_full = attn_full[:, :768], attn_full[:, 768:]
    attn_in, cot = rows[0].reshape(1024, WIDTH), rows[1].reshape(1024, WIDTH)

    projected = jnp.dot(attn_in, qkv_full, preferred_element_type=f32).astype(bf16)
    query_heads, key_heads, value_heads = (
        projected[:, 256 * t : 256 * t + 256].reshape(2, 512, 2, HEAD) for t in range(3)
    )
    scores = score_block(query_heads, key_heads, allowed)
    row_max = jnp.max(scores, axis=-1, keepdims=True)
    expd = jnp.exp(scores - row_max)
    row_sum = jnp.sum(expd, axis=-1, keepdims=True)
    log_total = row_max + jnp.log(row_sum)
    prob_low = (expd / row_sum).astype(bf16)
    attended = jnp.einsum("rhqk,rkhe->rqhe", prob_low, value_heads, preferred_element_type=f32)
    attended = attended.reshape(1024, 256).astype(bf16)
    partial_branch = jnp.einsum("sf,df->sd", attended, out_full, preferred_element_type=f32)
    branch, up_full = fused(
        [share_sum(partial_branch.astype(bf16)), weight_gather(own_up)], "0101111111", 3
    )
    up_full = up_full.reshape(WIDTH, PART)
    middle = inputs_share + branch
    normed_two, inv_two = standardize(middle)
    ffn_share = (normed_two * gain_two + shift_two).astype(bf16)
    ffn_in, down_full = fused([share_gather(ffn_share), weight_gather(own_down)], "0111101111", 4)
    ffn_in = ffn_in.reshape(1024, WIDTH)
    down_full = down_full.reshape(WIDTH, PART)
    up_proj = jnp.dot(ffn_in, up_full, preferred_element_type=f32)
    hidden = jax.nn.gelu(up_proj, approximate=True).astype(bf16)
    partial_ffn = jnp.einsum("sf,df->sd", hidden, down_full, preferred_element_type=f32)
    grad_w_down = jnp.einsum("sd,sf->df", cot, hidden, preferred_element_type=f32).astype(bf16)
    grad_hidden = jnp.dot(cot, down_full, preferred_element_type=f32)
    _, gelu_pull = jax.vjp(lambda value: jax.nn.gelu(value, approximate=True), up_proj)
    grad_up = gelu_pull(grad_hidden)[0].astype(bf16)
    grad_w_up = jnp.einsum("sd,sf->df", ffn_in, grad_up, preferred_element_type=f32).astype(bf16)
    partial_ffn_in = jnp.einsum("sf,df->sd", grad_up, up_full, preferred_element_type=f32)
    grad_ffn_in, ffn_out, sum_down = fused(
        [
            share_sum(partial_ffn_in.astype(bf16)),
            share_sum(partial_ffn.astype(bf16)),
            weight_sum(grad_w_down),
        ],
        "0201222011222",
        5,
        56,
    )
    layer_out = middle + ffn_out
    grad_norm_mid, grad_gain_two, grad_shift_two = norm_back(
        grad_ffn_in, normed_two, inv_two, gain_two
    )
    grad_middle = cot_share + grad_norm_mid
    grad_branch, sum_up = fused(
        [share_gather(grad_middle.astype(bf16)), weight_sum(grad_w_up)], "01111011", 6
    )
    grad_branch = grad_branch.reshape(1024, WIDTH)
    grad_w_out = jnp.einsum("sd,sf->df", grad_branch, attended, preferred_element_type=f32)
    grad_attended = jnp.dot(grad_branch, out_full, preferred_element_type=f32).astype(bf16)
    grad_att_heads = grad_attended.reshape(2, 512, 2, HEAD)
    again_scores = score_block(query_heads, key_heads, allowed)
    probs = jnp.exp(again_scores - log_total)
    probs_low = probs.astype(bf16)
    grad_probs = jnp.einsum(
        "rqhe,rkhe->rhqk", grad_att_heads, value_heads, preferred_element_type=f32
    )
    inner = jnp.sum(grad_probs * probs, axis=-1, keepdims=True)
    grad_scores = (probs * (grad_probs - inner)).astype(bf16)
    grad_query = jnp.einsum(
        "rhqk,rkhe->rqhe", grad_scores, key_heads, preferred_element_type=f32
    ) * HEAD ** (-0.5)
    grad_key = jnp.einsum(
        "rhqk,rqhe->rkhe", grad_scores, query_heads, preferred_element_type=f32
    ) * HEAD ** (-0.5)
    grad_value = jnp.einsum(
        "rhqk,rqhe->rkhe", probs_low, grad_att_heads, preferred_element_type=f32
    )
    grad_projected = jnp.concatenate(
        [g.reshape(1024, 256) for g in (grad_query, grad_key, grad_value)], axis=1
    ).astype(bf16)
    grad_w_qkv = jnp.einsum("sd,sf->df", attn_in, grad_projected, preferred_element_type=f32)
    partial_attn_in = jnp.einsum("sf,df->sd", grad_projected, qkv_full, preferred_element_type=f32)
    grad_w_attn = jnp.concatenate([grad_w_qkv.astype(bf16), grad_w_out.astype(bf16)], axis=1)
    grad_attn_in, sum_attn = fused(
        [share_sum(partial_attn_in.astype(bf16)), weight_sum(grad_w_attn)], "01011011", 7
    )
    grad_norm_in, grad_gain_one, grad_shift_one = norm_back(
        grad_attn_in, normed_one, inv_one, gain_one
    )
    input_grad = grad_middle + grad_norm_in

    sum_attn, sum_up, sum_down = (g.astype(f32) for g in (sum_attn, sum_up, sum_down))
    out_qkv = sum_attn[:, :, :768].reshape(2, 64, 3, 256).transpose(1, 2, 0, 3).reshape(64, 3, 512)
    out_out = sum_attn[:, :, 768:].transpose(1, 0, 2).reshape(64, 512)
    out_up = sum_up.transpose(1, 0, 2).reshape(64, WIDTH)
    out_down = sum_down.transpose(1, 0, 2).reshape(64, WIDTH)

    small = jnp.stack([grad_gain_one, grad_shift_one, grad_gain_two, grad_shift_two])
    small = jnp.pad(small.reshape(4, 32, 64).transpose(1, 0, 2), ((0, 0), (0, 4), (0, 64)))
    small = small_reduce(small, 10)[:4, :64]

    ends = jnp.stack([layer_out.astype(bf16), input_grad.astype(bf16)])
    (tokens,) = fused([row_gather(ends)], "000", 8)
    tokens = tokens.reshape(2, 1, 512, WIDTH).astype(f32)
    return (
        tokens[0],
        tokens[1],
        small[0],
        small[1],
        out_qkv,
        out_out,
        small[2],
        small[3],
        out_up,
        out_down,
    )


def solution(mesh):
    in_specs = (
        P("dp", None, None),
        P("dp", None),
        P("dp", None),
        P("dp", None),
        P(),
        P("dp"),
        P("dp"),
        P("dp", None, "mp"),
        P("dp", "mp"),
        P("dp"),
        P("dp"),
        P("dp", "mp"),
        P("dp", "mp"),
        P("dp", None, None),
    )
    out_specs = (
        P("dp", None, None),
        P("dp", None, None),
        P("dp"),
        P("dp"),
        P("dp", None, "mp"),
        P("dp", "mp"),
        P("dp"),
        P("dp"),
        P("dp", "mp"),
        P("dp", "mp"),
    )
    return jax.shard_map(
        on_device, mesh=mesh, in_specs=in_specs, out_specs=out_specs, check_vma=False
    )
```

time: 1180 us -> 510 us (0.43)
  the two profiles are of different devices: /device:TPU:16 before, /device:TPU:1 now
where the time goes in v2:
time: 510 us; the launch traced here: 503 us
  Pallas kernels  340 us (67%)
  matrix products  80.3 us (16%)
  local copies, waits for them, and re-layouts  61 us (12%)
  other arithmetic  19.7 us (4%)
    pallas_call x7, Pallas kernels, fused(): pl.pallas_call(functools.partial(fused_kernel, jobs, schedule), out_shape...  312 us
    pallas_call x1, Pallas kernels, small_reduce(): pl.pallas_call(small_reduce_kernel, out_shape=jax.ShapeDtypeStruct((8, 12...  15.3 us
    pallas_call x1, Pallas kernels, small_gather(): pl.pallas_call(small_gather_kernel, out_shape=(jax.ShapeDtypeStruct((32,...  12.4 us
    gather x1, local copies, waits for them, and re-layouts, on_device(): jnp.take(codebook, ids_half, axis=0).astype(f32)  11.4 us

profile of v2, /device:TPU:1, one launch (start us, length us, event | category | flops | bytes accessed | tf_op | source)
XLA Modules:
  0.0 502.6 jit_solution(1975463050213567948)
XLA Ops:
  4.4 12.4 %shard_map.213 = (f32[32,8,128]{2,1,0:T(8,128)S(1)}, f32[8,128]{1,0:T(8,128)S(1)}) custom-call(f32[8,128]{1,0:T(8,128)S(1)} %fusion.58.own, f32[8,128]{1,0:T(8,128)S(1)} %add_convert_fusion.3.mask), custom_call_target="tpu_custom_call" | custom-call | tf_op jit(solution)/shard_map/pallas_call | solution.py:169
  20.9 1.5 or_and_fusion
  22.3 11.4 %gather_fusion = bf16[256,2048]{1,0:T(8,128)(2,1)} fusion(bf16[4096,2048]{1,0:T(8,128)(2,1)} %param.18, s32[1024]{0:T(1024)S(1)} %pad_clamp_fusion), kind=kCustom, calls=%fused_computation | custom fusion | bytes 2098176 | tf_op jit(solution)/shard_map/jit(_take)/gather | solution.py:757
  33.8 2.2 fusion.64
  36.1 1.6 multiply_reduce_fusion.1
  38.7 48.3 %shard_map.214 = (bf16[2,2,2,2,128,2048]{5,4,3,2,1,0:T(8,128)(2,1)}, bf16[2,4,4,64,1024]{4,3,2,1,0:T(8,128)(2,1)}) custom-call(bf16[2,2,128,2048]{3,2,1,0:T(8,128)(2,1)S(1)} %pad_maximum_fusion.1.refs_0_, bf16[2,64,1024]{2,1,0:T(8,128)(2,1)S(1)} %pad_maximum_fusion.3.refs_1_), custom_call_target="tpu_custom_call" | custom-call | tf_op jit(solution)/shard_map/pallas_call | solution.py:118
  87.0 5.9 %fusion.66 = (bf16[1,2,2,2,128,2048]{5,4,3,2,1,0:T(8,128)(2,1)}, bf16[1,2,2,2,128,2048]{5,4,3,2,1,0:T(8,128)(2,1)S(1)}) fusion(bf16[2,2,2,2,128,2048]{5,4,3,2,1,0:T(8,128)(2,1)} %get-tuple-element.26), kind=kLoop, calls=%fused_computation.149 | loop fusion | bytes 16777216 | tf_op jit(solution)/shard_map/slice | solution.py:771
  93.2 3.5 fusion.22
  97.7 2.0 reshape.401
  100.7 1.3 copy.74
  102.0 2.0 reshape.402
  104.0 2.0 copy.77
  106.0 2.3 fusion.69
  108.9 1.4 copy-done.3
  110.2 1.7 fusion.33
  111.9 2.0 copy.69
  113.9 4.7 convolution_convert_fusion
  118.6 41.6 %shard_map.215 = (f32[128,2048]{1,0:T(8,128)S(1)}, bf16[2,4,4,64,1024]{4,3,2,1,0:T(8,128)(2,1)S(1)}) custom-call(bf16[2,2,2,128,2048]{4,3,2,1,0:T(8,128)(2,1)} %bitcast.172, bf16[2,64,1024]{2,1,0:T(8,128)(2,1)S(1)} %bitcast.164), custom_call_target="tpu_custom_call" | custom-call | tf_op jit(solution)/shard_map/pallas_call | solution.py:118
  161.0 47.5 %shard_map.216 = (bf16[2,2,2,128,2048]{4,3,2,1,0:T(8,128)(2,1)S(1)}, bf16[2,4,4,64,1024]{4,3,2,1,0:T(8,128)(2,1)}) custom-call(bf16[128,2048]{1,0:T(8,128)(2,1)S(1)} %add_convert_fusion.2.refs_0_, bf16[2,64,1024]{2,1,0:T(8,128)(2,1)S(1)} %bitcast.163), custom_call_target="tpu_custom_call" | custom-call | tf_op jit(solution)/shard_map/pallas_call | solution.py:118
  208.5 7.7 %fusion.70 = f32[1024,1024]{1,0:T(8,128)S(1)} fusion(bf16[1024,2048]{1,0:T(8,128)(2,1)} %bitcast.182, bf16[2048,1024]{1,0:T(8,128)(2,1)} %bitcast.216), kind=kOutput, calls=%fused_computation.153 | convolution fusion | flops 4294967296 | bytes 12582912 | tf_op jit(solution)/shard_map/dot_general | solution.py:800
  216.2 6.7 %fusion.6 = (bf16[1024,1024]{1,0:T(8,128)(2,1)S(1)}, f32[1024,1024]{1,0:T(8,128)S(1)}) fusion(f32[1024,1024]{1,0:T(8,128)S(1)} %fusion.70, bf16[1024,2048]{1,0:T(8,128)(2,1)S(1)} %bitcast.168, bf16[2048,1024]{1,0:T(8,128)(2,1)S(1)} %bitcast.166), kind=kOutput, calls=%fused_computation.9 | convolution fusion | flops 4315938816 | bytes 18874368 | tf_op jit(solution)/shard_map/dot_general | solution.py:796
  222.9 6.2 %convolution_convert_fusion.2 = bf16[2048,1024]{1,0:T(8,128)(2,1)} fusion(bf16[1024,2048]{1,0:T(8,128)(2,1)S(1)} %bitcast.169, bf16[1024,1024]{1,0:T(8,128)(2,1)S(1)} %get-tuple-element.76), kind=kOutput, calls=%fused_computation.20 | convolution fusion | flops 4297064448 | bytes 10485760 | tf_op jit(solution)/shard_map/sd,sf->df/dot_general | solution.py:803
  229.1 6.2 %convolution_convert_fusion.5 = bf16[1024,2048]{1,0:T(8,128)(2,1)} fusion(bf16[1024,1024]{1,0:T(8,128)(2,1)S(1)} %get-tuple-element.76, bf16[2048,1024]{1,0:T(8,128)(2,1)S(1)} %bitcast.167), kind=kOutput, calls=%fused_computation.23 | convolution fusion | flops 4297064448 | bytes 10485760 | tf_op jit(solution)/shard_map/sf,df->sd/dot_general | solution.py:804
  235.2 6.7 %convolution_convert_fusion.4 = bf16[1024,2048]{1,0:T(8,128)(2,1)} fusion(bf16[2048,1024]{1,0:T(8,128)(2,1)S(1)} %bitcast.217, f32[1024,1024]{1,0:T(8,128)S(1)} %get-tuple-element.77), kind=kOutput, calls=%fused_computation.22 | convolution fusion | flops 4306501632 | bytes 12582912 | tf_op jit(solution)/shard_map/sf,df->sd/dot_general | solution.py:798
  241.9 6.6 %convolution_convert_fusion.3 = bf16[2048,1024]{1,0:T(8,128)(2,1)} fusion(bf16[1024,2048]{1,0:T(8,128)(2,1)S(1)} %bitcast.183, f32[1024,1024]{1,0:T(8,128)S(1)} %get-tuple-element.77), kind=kOutput, calls=%fused_computation.21 | convolution fusion | flops 4306501632 | bytes 12582912 | tf_op jit(solution)/shard_map/sd,sf->df/dot_general | solution.py:799
  248.5 68.2 %shard_map.217 = (f32[128,2048]{1,0:T(8,128)}, f32[128,2048]{1,0:T(8,128)}, bf16[2,64,1024]{2,1,0:T(8,128)(2,1)}) custom-call(bf16[2,2,2,128,2048]{4,3,2,1,0:T(8,128)(2,1)} %bitcast.174, bf16[2,2,2,128,2048]{4,3,2,1,0:T(8,128)(2,1)} %bitcast.175, bf16[2,4,4,64,1024]{4,3,2,1,0:T(8,128)(2,1)} %bitcast.176), custom_call_target="tpu_custom_call" | custom-call | tf_op jit(solution)/shard_map/pallas_call | solution.py:118
  316.7 2.8 multiply_reduce_fusion.2
  319.6 1.7 fusion.62
  321.3 34.9 %shard_map.218 = (bf16[2,2,2,128,2048]{4,3,2,1,0:T(8,128)(2,1)S(1)}, bf16[2,64,1024]{2,1,0:T(8,128)(2,1)S(1)}) custom-call(bf16[128,2048]{1,0:T(8,128)(2,1)S(1)} %get-tuple-element.52.refs_0_, bf16[2,4,4,64,1024]{4,3,2,1,0:T(8,128)(2,1)} %bitcast.177), custom_call_target="tpu_custom_call" | custom-call | tf_op jit(solution)/shard_map/pallas_call | solution.py:118
  356.2 2.0 copy-done.1
  358.4 4.6 convolution_convert_fusion.7
  363.0 2.5 convolution_convert_fusion.8
  366.1 3.9 fusion.34
  370.0 2.2 copy.82
  374.0 3.2 multiply_reduce_fusion
  378.6 1.6 fusion.31
  380.3 1.3 fusion.32
  381.5 1.3 copy.76
  382.9 1.3 copy.79
  384.4 6.1 %convolution_convert_fusion.6 = bf16[2048,768]{0,1:T(8,128)(2,1)S(1)} fusion(bf16[1024,2048]{1,0:T(8,128)(2,1)} %bitcast.181, bf16[1024,768]{1,0:T(8,128)(2,1)S(1)} %bitcast_dynamic-update-slice_fusion), kind=kOutput, calls=%fused_computation.25 | convolution fusion | flops 3222798336 | bytes 8912896 | tf_op jit(solution)/shard_map/sd,sf->df/dot_general | solution.py:847
  390.6 5.0 convolution_convert_fusion.1
  395.6 2.3 pad_maximum_fusion
  397.9 6.4 %copy.83 = bf16[2048,1024]{1,0:T(8,128)(2,1)} copy(bf16[2048,1024]{0,1:T(8,128)(2,1)} %pad_maximum_fusion) | data formatting | bytes 8388608 | tf_op jit(solution)/shard_map/concatenate | solution.py:849
  404.3 2.2 copy-done
  406.5 42.3 %shard_map.219 = (f32[128,2048]{1,0:T(8,128)S(1)}, bf16[2,64,1024]{2,1,0:T(8,128)(2,1)S(1)}) custom-call(bf16[2,2,2,128,2048]{4,3,2,1,0:T(8,128)(2,1)S(1)} %bitcast.162, bf16[2,4,4,64,1024]{4,3,2,1,0:T(8,128)(2,1)} %bitcast.173), custom_call_target="tpu_custom_call" | custom-call | tf_op jit(solution)/shard_map/pallas_call | solution.py:118
  450.2 15.3 %shard_map.221 = f32[8,128]{1,0:T(8,128)S(1)} custom-call(f32[32,8,128]{2,1,0:T(8,128)S(1)} %pad.12.pieces), custom_call_target="tpu_custom_call" | custom-call | tf_op jit(solution)/shard_map/pallas_call | solution.py:225
  468.4 29.3 %shard_map.220 = bf16[2,2,2,128,2048]{4,3,2,1,0:T(8,128)(2,1)S(1)} custom-call(bf16[2,128,2048]{2,1,0:T(8,128)(2,1)S(1)} %pad_maximum_fusion.2.refs_0_), custom_call_target="tpu_custom_call" | custom-call | tf_op jit(solution)/shard_map/pallas_call | solution.py:118
  497.7 4.5 fusion.67
  (114 shorter events, 20.6 us)
Async XLA Ops:
  22.3 11.4 %copy-start.17 = (bf16[1,512,2048]{2,1,0:T(8,128)(2,1)S(1)}, bf16[1,512,2048]{2,1,0:T(8,128)(2,1)}, u32[]{:S(2)}) copy-start(bf16[1,512,2048]{2,1,0:T(8,128)(2,1)} %param.27) | copy-start | bytes 6291460
  33.8 3.9 copy-start.5
  33.8 3.9 copy-start.14
  87.0 6.2 %copy-start.19 = (bf16[2,4,4,64,1024]{4,3,2,1,0:T(8,128)(2,1)S(1)}, bf16[2,4,4,64,1024]{4,3,2,1,0:T(8,128)(2,1)}, u32[]{:S(2)}) copy-start(bf16[2,4,4,64,1024]{4,3,2,1,0:T(8,128)(2,1)} %get-tuple-element.27) | copy-start | bytes 12582916
  92.9 3.7 copy-start.9
  106.0 4.3 copy-start.12
  108.3 2.0 copy-start.3
  229.1 6.2 %copy-start.22 = (bf16[2,4,4,64,1024]{4,3,2,1,0:T(8,128)(2,1)S(1)}, bf16[2,4,4,64,1024]{4,3,2,1,0:T(8,128)(2,1)}, u32[]{:S(2)}) copy-start(bf16[2,4,4,64,1024]{4,3,2,1,0:T(8,128)(2,1)} %get-tuple-element.30) | copy-start | bytes 12582916
  235.2 6.7 %copy-start.10 = (bf16[1,2,2,2,128,2048]{5,4,3,2,1,0:T(8,128)(2,1)S(1)}, bf16[1,2,2,2,128,2048]{5,4,3,2,1,0:T(8,128)(2,1)}, u32[]{:S(2)}) copy-start(bf16[1,2,2,2,128,2048]{5,4,3,2,1,0:T(8,128)(2,1)} %get-tuple-element.62) | copy-start | bytes 12582916
  316.7 2.9 copy-start.8
  319.6 38.8 %copy-start.11 = (bf16[2,512,2,128]{3,2,1,0:T(2,128)(2,1)S(1)}, bf16[2,512,2,128]{3,2,1,0:T(2,128)(2,1)}, u32[]{:S(2)}) copy-start(bf16[2,512,2,128]{3,2,1,0:T(2,128)(2,1)} %copy.69) | copy-start | bytes 1572868
  356.2 2.0 copy-start.1
  358.4 4.6 copy-start.2
  366.0 7.0 %copy-start.21 = (bf16[2,64,1024]{2,1,0:T(8,128)(2,1)S(1)}, bf16[2,64,1024]{2,1,0:T(8,128)(2,1)}, u32[]{:S(2)}) copy-start(bf16[2,64,1024]{2,1,0:T(8,128)(2,1)} %get-tuple-element.39) | copy-start | bytes 786436
  366.1 7.9 %copy-start.13 = (bf16[2,512,2,128]{3,2,1,0:T(2,128)(2,1)S(1)}, bf16[2,512,2,128]{3,2,1,0:T(2,128)(2,1)}, u32[]{:S(2)}) copy-start(bf16[2,512,2,128]{3,2,1,0:T(2,128)(2,1)} %reshape.401) | copy-start | bytes 1572868
  374.0 3.4 copy-start.4
  377.4 1.2 copy-start.7
  380.3 4.1 copy-start.16
  384.4 6.1 %copy-start.20 = (bf16[2,4,4,64,1024]{4,3,2,1,0:T(8,128)(2,1)S(1)}, bf16[2,4,4,64,1024]{4,3,2,1,0:T(8,128)(2,1)}, u32[]{:S(2)}) copy-start(bf16[2,4,4,64,1024]{4,3,2,1,0:T(8,128)(2,1)} %get-tuple-element.27) | copy-start | bytes 12582916
  390.5 5.0 copy-start.18
  404.3 2.2 copy-start
  406.5 42.3 %copy-start.6 = (f32[256,2048]{1,0:T(8,128)S(1)}, f32[256,2048]{1,0:T(8,128)}, u32[]{:S(2)}) copy-start(f32[256,2048]{1,0:T(8,128)} %get-tuple-element.57) | copy-start | bytes 6291460
  448.8 1.0 copy-start.15

commit v3 on v2

--- a/solution.py
+++ b/solution.py
@@ -94,6 +94,58 @@
 }
 
 
+def dp_peer(step):
+    return (lax.rem(lax.axis_index("dp") + step, 32), lax.axis_index("mp"))
+
+
+def mp_peer(step):
+    return (lax.axis_index("dp"), lax.rem(lax.axis_index("mp") + step, 4))
+
+
+PEERS.update({f"dp{k}": functools.partial(dp_peer, k) for k in range(1, 32)})
+PEERS.update({f"mp{k}": functools.partial(mp_peer, k) for k in range(1, 4)})
+DP = [f"dp{k}" for k in range(1, 32)]
+MP = ["mp1", "mp2", "mp3"]
+
+
+def kernel_call(body, jobs, peers, ins, outs, scratch, collective_id, mib=56):
+    def kernel(*refs):
+        taken = 0
+
+        def take(count):
+            nonlocal taken
+            taken += count
+            return refs[taken - count : taken]
+
+        groups = [take(len(ins)), take(len(outs)), take(len(scratch))]
+        makers = []
+        for job in jobs:
+            own = take(len(job["scratch"]))
+            makers.append(lambda *given, job=job, own=own: job["steps"](*given, *own))
+        greet([PEERS[name]() for name in peers])
+        body(*groups, makers)
+
+    return pl.pallas_call(
+        kernel,
+        out_shape=[shape for shape, _ in outs],
+        in_specs=[spec for _, spec in ins],
+        out_specs=[spec for _, spec in outs],
+        scratch_shapes=scratch + [one for job in jobs for one in job["scratch"]],
+        compiler_params=params(collective_id, mib),
+    )(*[array for array, _ in ins])
+
+
+def finish(*runs):
+    for run in runs:
+        for _ in run:
+            pass
+
+
+def step(*runs):
+    for run in runs:
+        next(run, None)
+
+
 def fused_kernel(jobs, schedule, *refs):
     taken = 0
 
@@ -130,104 +182,75 @@
     return jax.ShapeDtypeStruct(shape, dtype)
 
 
-def small_gather_kernel(own, mask, everyone, mask_out, send, recv, mask_send, mask_recv):
-    dp, mp = lax.axis_index("dp"), lax.axis_index("mp")
-    barrier = pltpu.get_barrier_semaphore()
-
-    def greet_one(k, carry):
-        pl.semaphore_signal(
-            barrier, inc=1, device_id=(lax.rem(dp + k, 32), mp), device_id_type=MESH
-        )
-        return carry
-
-    lax.fori_loop(1, 32, greet_one, 0)
-    pl.semaphore_wait(barrier, 31)
-
-    def move(k):
-        peer = lax.rem(dp + k, 32)
-        return remote(own, everyone.at[dp], send.at[k], recv.at[dp], (peer, mp))
-
-    def start(k, carry):
-        move(k).start()
-        return carry
-
-    def finish(k, carry):
-        source = lax.rem(dp + k, 32)
-        move(k).wait_send()
-        remote(own, everyone.at[source], send.at[k], recv.at[source], (source, mp)).wait_recv()
-        return carry
-
-    swap = remote(mask, mask_out, mask_send, mask_recv, lo_partner())
-    swap.start()
-    lax.fori_loop(1, 32, start, 0)
-    everyone[dp] = own[...]
-    lax.fori_loop(1, 32, finish, 0)
-    swap.wait()
-
-
-def small_gather(own, mask, collective_id):
-    return pl.pallas_call(
-        small_gather_kernel,
-        out_shape=(
-            jax.ShapeDtypeStruct((32, 8, 128), f32),
-            jax.ShapeDtypeStruct((8, 128), f32),
-        ),
-        in_specs=[VMEM, VMEM],
-        out_specs=(VMEM, VMEM),
-        scratch_shapes=[sems(32), sems(32), pltpu.SemaphoreType.DMA, pltpu.SemaphoreType.DMA],
-        compiler_params=params(collective_id, 8),
-    )(own, mask)
-
-
-def small_reduce_kernel(pieces, out, arrived, summed, more, send, recv, send_two, recv_two):
-    dp, mp = lax.axis_index("dp"), lax.axis_index("mp")
-    barrier = pltpu.get_barrier_semaphore()
-
-    def greet_one(k, carry):
-        pl.semaphore_signal(
-            barrier, inc=1, device_id=(lax.rem(dp + k, 32), mp), device_id_type=MESH
-        )
-        return carry
-
-    lax.fori_loop(1, 32, greet_one, 0)
-    for k in (1, 2, 3):
-        pl.semaphore_signal(
-            barrier, inc=1, device_id=(dp, lax.rem(mp + k, 4)), device_id_type=MESH
-        )
-    pl.semaphore_wait(barrier, 34)
-
-    def move(k):
-        peer = lax.rem(dp + k, 32)
-        return remote(pieces.at[peer], arrived.at[k], send.at[k], recv.at[k], (peer, mp))
-
-    def start(k, carry):
-        move(k).start()
-        return carry
-
-    def finish(k, total):
-        move(k).wait()
-        return total + arrived[k]
-
-    lax.fori_loop(1, 32, start, 0)
-    summed[...] = lax.fori_loop(1, 32, finish, pieces[dp])
-    copies = [
-        remote(summed, more.at[k - 1], send_two.at[k], recv_two.at[k], (dp, lax.rem(mp + k, 4)))
-        for k in (1, 2, 3)
-    ]
-    for copy in copies:
-        copy.start()
-    for copy in copies:
-        copy.wait()
-    out[...] = summed[...] + more[0] + more[1] + more[2]
-
-
-def small_reduce(pieces, collective_id):
-    return pl.pallas_call(
-        small_reduce_kernel,
-        out_shape=jax.ShapeDtypeStruct((8, 128), f32),
-        in_specs=[VMEM],
-        out_specs=VMEM,
-        scratch_shapes=[
+def small_gather():
+    def steps(own, mask, everyone, mask_out, mask_send, mask_recv, send, recv):
+        dp, mp = lax.axis_index("dp"), lax.axis_index("mp")
+
+        def move(k):
+            return remote(own, everyone.at[dp], send.at[k], recv.at[dp], dp_peer(k))
+
+        def start(k, carry):
+            move(k).start()
+            return carry
+
+        swap = remote(mask, mask_out, mask_send, mask_recv, lo_partner())
+        swap.start()
+        lax.fori_loop(1, 32, start, 0)
+        everyone[dp] = own[...]
+        yield
+
+        def end(k, carry):
+            source = lax.rem(dp + k, 32)
+            move(k).wait_send()
+            remote(own, everyone.at[source], send.at[k], recv.at[source], dp_peer(k)).wait_recv()
+            return carry
+
+        lax.fori_loop(1, 32, end, 0)
+        swap.wait()
+
+    return {
+        "scratch": [pltpu.SemaphoreType.DMA] * 2 + [sems(32), sems(32)],
+        "peers": DP,
+        "steps": steps,
+    }
+
+
+def small_reduce(rows):
+    def steps(rows, out, arrived, summed, more, send, recv, send_two, recv_two):
+        dp = lax.axis_index("dp")
+
+        def move(k):
+            tile = lax.div(lax.rem(dp + k, 32), 2)
+            src = rows.at[:, pl.ds(pl.multiple_of(tile * 128, 128), 128)]
+            return remote(src, arrived.at[k], send.at[k], recv.at[k], dp_peer(k))
+
+        def start(k, carry):
+            move(k).start()
+            return carry
+
+        def add(k, total):
+            move(k).wait()
+            return total + arrived[k]
+
+        lax.fori_loop(1, 32, start, 0)
+        yield
+        mine = rows[:, pl.ds(pl.multiple_of(lax.div(dp, 2) * 128, 128), 128)]
+        summed[...] = lax.fori_loop(1, 32, add, mine)
+        copies = [
+            remote(summed, more.at[k - 1], send_two.at[k], recv_two.at[k], mp_peer(k))
+            for k in (1, 2, 3)
+        ]
+        for copy in copies:
+            copy.start()
+        yield
+        for copy in copies:
+            copy.wait()
+        out[...] = summed[...] + more[0] + more[1] + more[2]
+
+    return {
+        "ins": [(rows, VMEM)],
+        "outs": [(shaped(f32, 8, 128), VMEM)],
+        "scratch": [
             pltpu.VMEM((32, 8, 128), f32),
             pltpu.VMEM((8, 128), f32),
             pltpu.VMEM((3, 8, 128), f32),
@@ -236,12 +259,14 @@
             sems(4),
             sems(4),
         ],
-        compiler_params=params(collective_id, 8),
-    )(pieces)
-
-
-def row_exchange(halves):
-    count = halves.shape[0]
+        "peers": DP + MP,
+        "steps": steps,
+    }
+
+
+def row_exchange(halves=None, count=1):
+    if halves is not None:
+        count = halves.shape[0]
 
     def steps(halves, full, local_sem, send, recv):
         ylo, x, z, yhi, core = place()
@@ -284,7 +309,7 @@
             copy.wait()
 
     return {
-        "ins": [(halves, ANY)],
+        "ins": [(halves, VMEM)],
         "outs": [(shaped(bf16, count, 2, 2, 2, SHARE, WIDTH), ANY)],
         "scratch": [sems(count), sems(count, 5), sems(count, 5)],
         "peers": ["y1", "y3", "core"],
@@ -292,7 +317,7 @@
     }
 
 
-def share_gather(share):
+def share_gather(share=None):
     def steps(share, full, local_sem, send, recv):
         ylo, x, z, yhi, core = place()
         y = yhi * 2 + ylo
@@ -326,7 +351,7 @@
         local.wait()
 
     return {
-        "ins": [(share, ANY)],
+        "ins": [(share, VMEM)],
         "outs": [(shaped(bf16, 2, 2, 2, SHARE, WIDTH), ANY)],
         "scratch": [pltpu.SemaphoreType.DMA, sems(7), sems(7)],
         "peers": ["y1", "y2", "y3", "core"],
@@ -342,7 +367,7 @@
     lax.fori_loop(0, count // 16, body, 0)
 
 
-def share_sum(partial):
+def share_sum(partial=None, split=False):
     def steps(partial, out, from_core, turned, arrived, send, recv, send_two, recv_two):
         ylo, x, z, yhi, core = place()
         y = yhi * 2 + ylo
@@ -352,23 +377,38 @@
             target = ring(y, k)
             return partial.at[lax.rem(target, 2), half, lax.div(target, 2)]
 
-        first = {}
-        for k in (2, 1, 3, 0):
-            first[k] = remote(block(k, 1 - core), from_core.at[k], send.at[k], recv.at[k], other)
-            first[k].start()
-        yield
-        second = {}
-        for k in (2, 1, 3):
-            first[k].wait_recv()
-            mine = block(k, core)
-
-            def add(rows):
-                value = mine[rows].astype(f32) + from_core[k, rows].astype(f32)
-                turned[k, rows] = value.astype(bf16)
-
-            add_rows(SHARE, add)
-            second[k] = remote(turned.at[k], arrived.at[k], send_two.at[k], recv_two.at[k], y_peer(k))
-            second[k].start()
+        first, second = {}, {}
+
+        def to_core(order):
+            for k in order:
+                first[k] = remote(block(k, 1 - core), from_core.at[k], send.at[k], recv.at[k], other)
+                first[k].start()
+
+        def to_owner(order):
+            for k in order:
+                first[k].wait_recv()
+                mine = block(k, core)
+
+                def add(rows):
+                    value = mine[rows].astype(f32) + from_core[k, rows].astype(f32)
+                    turned[k, rows] = value.astype(bf16)
+
+                add_rows(SHARE, add)
+                second[k] = remote(
+                    turned.at[k], arrived.at[k], send_two.at[k], recv_two.at[k], y_peer(k)
+                )
+                second[k].start()
+
+        to_core((1, 3))
+        if not split:
+            to_core((2, 0))
+        yield
+        to_owner((1, 3))
+        yield
+        if split:
+            to_core((2, 0))
+            yield
+        to_owner((2,))
         yield
         first[0].wait_recv()
         for k in (1, 3, 2):
@@ -388,7 +428,7 @@
             second[k].wait_send()
 
     return {
-        "ins": [(partial.reshape(2, 2, 2, SHARE, WIDTH), VMEM)],
+        "ins": [(None if partial is None else partial.reshape(2, 2, 2, SHARE, WIDTH), VMEM)],
         "outs": [(shaped(f32, SHARE, WIDTH), VMEM)],
         "scratch": [pltpu.VMEM((4, SHARE, WIDTH), bf16)] * 3 + [sems(4)] * 4,
         "peers": ["y1", "y2", "y3", "core"],
@@ -423,7 +463,7 @@
         local.wait()
 
     return {
-        "ins": [(share, ANY)],
+        "ins": [(share, VMEM)],
         "outs": [(shaped(bf16, count, 2, 2, SHARE, WIDTH), ANY)],
         "scratch": [pltpu.SemaphoreType.DMA, sems(3), sems(3)],
         "peers": ["y2", "core"],
@@ -439,7 +479,7 @@
     return [[xz_neighbour(axis, d) for d in SIGNS] for axis in (0, 1)]
 
 
-def weight_gather(own):
+def weight_gather(own=None):
     def steps(own, full, local_sem, swap_send, swap_recv, send, recv):
         ylo, x, z, yhi, core = place()
         near = xz_near()
@@ -530,7 +570,7 @@
         local.wait()
 
     return {
-        "ins": [(own, ANY)],
+        "ins": [(own, VMEM)],
         "outs": [(shaped(bf16, 2, 4, 4, 64, PART), ANY)],
         "scratch": [pltpu.SemaphoreType.DMA] * 3 + [sems(64), sems(64)],
         "peers": XZ + ["y1", "y3"],
@@ -681,6 +721,232 @@
     }
 
 
+CODES = 4096
+CODE_CHUNK = 512
+
+
+def embed_body(ins, outs, scratch, makers):
+    ids, stream, cot, codebook, own_attn, norms, masks = ins
+    attn_full, cot_full, inputs_share, gains, masks_out, attn_weight = outs
+    everyone, chunk, total, halves, chunk_sem = scratch
+    make_small, make_gather, make_cot, make_attn = makers
+    ylo, x, z, yhi, core = place()
+    small = make_small(norms, masks, everyone, masks_out)
+    gather = make_gather(own_attn, attn_weight)
+    cot_move = make_cot(cot, cot_full)
+    attn_move = make_attn(halves, attn_full)
+
+    def fetch(j):
+        rows = pl.ds(j * CODE_CHUNK, CODE_CHUNK)
+        return pltpu.make_async_copy(codebook.at[rows], chunk.at[j % 2], chunk_sem.at[j % 2])
+
+    step(small, gather)
+    fetch(0).start()
+    step(cot_move)
+    total[...] = stream[...].astype(f32)
+    count = CODES // CODE_CHUNK
+    for j in range(count):
+        if j + 1 < count:
+            fetch(j + 1).start()
+        fetch(j).wait()
+        code = lax.broadcasted_iota(jnp.int32, (256, CODE_CHUNK), 1) + j * CODE_CHUNK
+        pick = jnp.where(ids[...] == code, 1.0, 0.0).astype(bf16)
+        for part in range(2):
+            columns = pl.ds(part * 1024, 1024)
+            total[:, columns] += jnp.dot(
+                pick, chunk[j % 2, :, columns], preferred_element_type=f32
+            )
+        if j in (2, 4, 6):
+            step(gather)
+    step(small)
+    for t in range(16):
+        for k in range(4):
+            pair = everyone[2 * t, pl.ds(k, 1)] + everyone[2 * t + 1, pl.ds(k, 1)]
+            gains[pl.ds(k, 1), pl.ds(128 * t, 128)] = pair
+    gain, shift = gains[pl.ds(0, 1)], gains[pl.ds(1, 1)]
+    for u in range(2):
+
+        def norm(i, carry):
+            at = pl.multiple_of(i * 16, 16)
+            value = total[pl.ds(u * SHARE + at, 16)]
+            normed, _ = standardize(value)
+            halves[0, u, pl.ds(at, 16)] = (normed * gain + shift).astype(bf16)
+            return carry
+
+        lax.fori_loop(0, SHARE // 16, norm, 0)
+    step(attn_move, gather)
+
+    def keep(i, carry):
+        at = pl.multiple_of(i * 16, 16)
+        inputs_share[pl.ds(at, 16)] = total[pl.ds(pl.multiple_of(yhi * SHARE + at, 16), 16)]
+        return carry
+
+    lax.fori_loop(0, SHARE // 16, keep, 0)
+    step(gather, gather, cot_move, gather, gather, attn_move, gather)
+    finish(attn_move, cot_move, gather)
+
+
+def embed(ids, stream, cot, codebook, own_attn, norms, masks, collective_id):
+    return kernel_call(
+        embed_body,
+        [small_gather(), weight_gather(), row_exchange(), row_exchange()],
+        DP + ["y1", "y3", "core"],
+        [
+            (ids, VMEM),
+            (stream, VMEM),
+            (cot, VMEM),
+            (codebook, ANY),
+            (own_attn, VMEM),
+            (norms, VMEM),
+            (masks, VMEM),
+        ],
+        [
+            (shaped(bf16, 1, 2, 2, 2, SHARE, WIDTH), ANY),
+            (shaped(bf16, 1, 2, 2, 2, SHARE, WIDTH), ANY),
+            (shaped(f32, SHARE, WIDTH), VMEM),
+            (shaped(f32, 8, WIDTH), VMEM),
+            (shaped(f32, 8, 128), VMEM),
+            (shaped(bf16, 2, 4, 4, 64, PART), ANY),
+        ],
+        [
+            pltpu.VMEM((32, 8, 128), f32),
+            pltpu.VMEM((2, CODE_CHUNK, WIDTH), bf16),
+            pltpu.VMEM((256, WIDTH), f32),
+            pltpu.VMEM((1, 2, SHARE, WIDTH), bf16),
+            sems(2),
+        ],
+        collective_id,
+    )
+
+
+TURNED = (((1,), (1,)), ((), ()))
+
+
+def turned_dot(a, b):
+    return lax.dot_general(a, b, TURNED, preferred_element_type=f32)
+
+
+def attention_body(ins, outs, scratch, makers):
+    attn_in, weight, mask, inputs_share, gains, own_up, own_down = ins
+    projected, attended, middle, ffn_full, up_full, down_full = outs
+    partial, branch, ffn_share = scratch
+    make_up, make_down, make_sum, make_share = makers
+    ylo, x, z, yhi, core = place()
+    up, down = make_up(own_up, up_full), make_down(own_down, down_full)
+    total = make_sum(partial, branch)
+    spread = make_share(ffn_share, ffn_full)
+
+    def project(r):
+        def one(t, carry):
+            columns = pl.ds(pl.multiple_of(t * 256, 256), 256)
+            projected[pl.ds(r * 512, 512), columns] = jnp.dot(
+                attn_in[pl.ds(r * 512, 512)], weight[:, columns], preferred_element_type=f32
+            ).astype(bf16)
+            return carry
+
+        lax.fori_loop(0, 3, one, 0)
+
+    def attend(r):
+        for h in range(2):
+            key = projected[pl.ds(r * 512, 512), pl.ds(256 + h * HEAD, HEAD)]
+            value = projected[pl.ds(r * 512, 512), pl.ds(512 + h * HEAD, HEAD)]
+
+            def one(q, carry):
+                rows = pl.ds(pl.multiple_of(r * 512 + q * 128, 128), 128)
+                query = projected[rows, pl.ds(h * HEAD, HEAD)]
+                scores = turned_dot(query, key) * HEAD ** (-0.5)
+                seen = mask[r, pl.ds(pl.multiple_of(q * 128, 128), 128)].astype(f32)
+                scores = jnp.where(seen > 0.5, scores, masked_score)
+                expd = jnp.exp(scores - jnp.max(scores, axis=-1, keepdims=True))
+                probs = expd / jnp.sum(expd, axis=-1, keepdims=True)
+                attended[rows, pl.ds(h * HEAD, HEAD)] = jnp.dot(
+                    probs.astype(bf16), value, preferred_element_type=f32
+                ).astype(bf16)
+                return carry
+
+            lax.fori_loop(0, 4, one, 0)
+
+    def send_out(r):
+        def one(n, carry):
+            columns = pl.ds(pl.multiple_of(n * 512, 512), 512)
+            out_weight = weight[columns, pl.ds(768, 256)]
+            for q in range(4):
+                rows = pl.ds(pl.multiple_of(r * 512 + q * 128, 128), 128)
+                partial[r, q // 2, q % 2, :, columns] = turned_dot(
+                    attended[rows], out_weight
+                ).astype(bf16)
+            return carry
+
+        lax.fori_loop(0, 4, one, 0)
+
+    step(up, down)
+    project(1 - ylo)
+    step(up, down)
+    attend(1 - ylo)
+    step(up, down)
+    send_out(1 - ylo)
+    step(total)
+    step(up, down)
+    project(ylo)
+    step(total)
+    step(up, down)
+    attend(ylo)
+    step(up, down)
+    send_out(ylo)
+    step(total)
+    step(up, down)
+    step(total)
+    step(up, down)
+    step(up, down)
+    finish(total)
+    gain, shift = gains[pl.ds(2, 1)], gains[pl.ds(3, 1)]
+
+    def norm(i, carry):
+        rows = pl.ds(pl.multiple_of(i * 16, 16), 16)
+        value = inputs_share[rows] + branch[rows]
+        middle[rows] = value
+        normed, _ = standardize(value)
+        ffn_share[rows] = (normed * gain + shift).astype(bf16)
+        return carry
+
+    lax.fori_loop(0, SHARE // 16, norm, 0)
+    step(spread)
+    step(up, down)
+    step(spread)
+    finish(spread, up, down)
+
+
+def attention(attn_in, weight, mask, inputs_share, gains, own_up, own_down, collective_id):
+    return kernel_call(
+        attention_body,
+        [weight_gather(), weight_gather(), share_sum(split=True), share_gather()],
+        XZ + ["y1", "y2", "y3", "core"],
+        [
+            (attn_in, VMEM),
+            (weight, VMEM),
+            (mask, VMEM),
+            (inputs_share, VMEM),
+            (gains, VMEM),
+            (own_up, VMEM),
+            (own_down, VMEM),
+        ],
+        [
+            (shaped(bf16, 1024, 768), VMEM),
+            (shaped(bf16, 1024, 256), VMEM),
+            (shaped(f32, SHARE, WIDTH), VMEM),
+            (shaped(bf16, 2, 2, 2, SHARE, WIDTH), ANY),
+            (shaped(bf16, 2, 4, 4, 64, PART), ANY),
+            (shaped(bf16, 2, 4, 4, 64, PART), ANY),
+        ],
+        [
+            pltpu.VMEM((2, 2, 2, SHARE, WIDTH), bf16),
+            pltpu.VMEM((SHARE, WIDTH), f32),
+            pltpu.VMEM((SHARE, WIDTH), bf16),
+        ],
+        collective_id,
+    )
+
+
 def standardize(value):
     mean = jnp.mean(value, axis=-1, keepdims=True)
     centered = value - mean
@@ -744,55 +1010,41 @@
     own_down = w_down.reshape(64, 2, PART).transpose(1, 0, 2)
 
     norms = jnp.stack([norm1_gain, norm1_shift, norm2_gain, norm2_shift]).astype(f32)
+    none = jnp.zeros_like(norms)
+    odd = lax.rem(z, 2) == 1
+    norms = jnp.concatenate([jnp.where(odd, none, norms), jnp.where(odd, norms, none)], axis=1)
     masks = jnp.concatenate([segment_ids.reshape(4, 128), padding.reshape(4, 128)]).astype(f32)
-    norms_all, masks_other = small_gather(jnp.pad(norms, ((0, 4), (0, 64))), masks, 1)
-    norms_all = norms_all[:, :4, :64].transpose(1, 0, 2).reshape(4, WIDTH)
-    gain_one, shift_one, gain_two, shift_two = norms_all
-    both = jnp.where(ylo == 0, jnp.stack([masks, masks_other]), jnp.stack([masks_other, masks]))
-    allowed = visible(both[:, :4].reshape(2, 512), both[:, 4:].reshape(2, 512))
-
     ids_half = lax.dynamic_slice_in_dim(code_ids[0], core * 256, 256, 0)
     stream_half = lax.dynamic_slice_in_dim(stream[0], core * 256, 256, 0)
     cot_half = lax.dynamic_slice_in_dim(cotangent[0], core * 256, 256, 0)
-    inputs_half = stream_half.astype(f32) + jnp.take(codebook, ids_half, axis=0).astype(f32)
-    normed_half, inv_half = standardize(inputs_half)
-    attn_half = (normed_half * gain_one + shift_one).astype(bf16)
-
-    def share_of(value):
-        return lax.dynamic_slice_in_dim(value, yhi * SHARE, SHARE, 0)
-
-    inputs_share, normed_one, inv_one = (share_of(v) for v in (inputs_half, normed_half, inv_half))
-    cot_share = share_of(cot_half).astype(f32)
-
-    halves = jnp.stack([attn_half, cot_half]).reshape(2, 2, SHARE, WIDTH)
-    rows, attn_full = fused([row_exchange(halves), weight_gather(own_attn)], "0111101111", 2)
+    attn_in, cot, inputs_share, gains, masks_other, attn_full = embed(
+        ids_half[:, None],
+        stream_half,
+        cot_half.reshape(1, 2, SHARE, WIDTH),
+        codebook,
+        own_attn,
+        jnp.pad(norms, ((0, 4), (0, 0))),
+        masks,
+        0,
+    )
+    gain_one, shift_one, gain_two, shift_two = (gains[k] for k in range(4))
+    attn_in, cot = attn_in.reshape(1024, WIDTH), cot.reshape(1024, WIDTH)
     attn_full = attn_full.reshape(WIDTH, PART)
     qkv_full, out_full = attn_full[:, :768], attn_full[:, 768:]
-    attn_in, cot = rows[0].reshape(1024, WIDTH), rows[1].reshape(1024, WIDTH)
-
-    projected = jnp.dot(attn_in, qkv_full, preferred_element_type=f32).astype(bf16)
+    both = jnp.where(ylo == 0, jnp.stack([masks, masks_other]), jnp.stack([masks_other, masks]))
+    allowed = visible(both[:, :4].reshape(2, 512), both[:, 4:].reshape(2, 512))
+    cot_share = lax.dynamic_slice_in_dim(cot_half, yhi * SHARE, SHARE, 0).astype(f32)
+    normed_one, inv_one = standardize(inputs_share)
+
+    projected, attended, middle, ffn_in, up_full, down_full = attention(
+        attn_in, attn_full, allowed.astype(bf16), inputs_share, gains, own_up, own_down, 1
+    )
     query_heads, key_heads, value_heads = (
         projected[:, 256 * t : 256 * t + 256].reshape(2, 512, 2, HEAD) for t in range(3)
     )
-    scores = score_block(query_heads, key_heads, allowed)
-    row_max = jnp.max(scores, axis=-1, keepdims=True)
-    expd = jnp.exp(scores - row_max)
-    row_sum = jnp.sum(expd, axis=-1, keepdims=True)
-    log_total = row_max + jnp.log(row_sum)
-    prob_low = (expd / row_sum).astype(bf16)
-    attended = jnp.einsum("rhqk,rkhe->rqhe", prob_low, value_heads, preferred_element_type=f32)
-    attended = attended.reshape(1024, 256).astype(bf16)
-    partial_branch = jnp.einsum("sf,df->sd", attended, out_full, preferred_element_type=f32)
-    branch, up_full = fused(
-        [share_sum(partial_branch.astype(bf16)), weight_gather(own_up)], "0101111111", 3
-    )
-    up_full = up_full.reshape(WIDTH, PART)
-    middle = inputs_share + branch
     normed_two, inv_two = standardize(middle)
-    ffn_share = (normed_two * gain_two + shift_two).astype(bf16)
-    ffn_in, down_full = fused([share_gather(ffn_share), weight_gather(own_down)], "0111101111", 4)
     ffn_in = ffn_in.reshape(1024, WIDTH)
-    down_full = down_full.reshape(WIDTH, PART)
+    up_full, down_full = up_full.reshape(WIDTH, PART), down_full.reshape(WIDTH, PART)
     up_proj = jnp.dot(ffn_in, up_full, preferred_element_type=f32)
     hidden = jax.nn.gelu(up_proj, approximate=True).astype(bf16)
     partial_ffn = jnp.einsum("sf,df->sd", hidden, down_full, preferred_element_type=f32)
@@ -808,7 +1060,7 @@
             share_sum(partial_ffn.astype(bf16)),
             weight_sum(grad_w_down),
         ],
-        "0201222011222",
+        "200122222",
         5,
         56,
     )
@@ -818,14 +1070,14 @@
     )
     grad_middle = cot_share + grad_norm_mid
     grad_branch, sum_up = fused(
-        [share_gather(grad_middle.astype(bf16)), weight_sum(grad_w_up)], "01111011", 6
+        [share_gather(grad_middle.astype(bf16)), weight_sum(grad_w_up)], "10111111", 6
     )
     grad_branch = grad_branch.reshape(1024, WIDTH)
     grad_w_out = jnp.einsum("sd,sf->df", grad_branch, attended, preferred_element_type=f32)
     grad_attended = jnp.dot(grad_branch, out_full, preferred_element_type=f32).astype(bf16)
     grad_att_heads = grad_attended.reshape(2, 512, 2, HEAD)
     again_scores = score_block(query_heads, key_heads, allowed)
-    probs = jnp.exp(again_scores - log_total)
+    probs = jax.nn.softmax(again_scores, axis=-1)
     probs_low = probs.astype(bf16)
     grad_probs = jnp.einsum(
         "rqhe,rkhe->rhqk", grad_att_heads, value_heads, preferred_element_type=f32
@@ -848,7 +1100,7 @@
     partial_attn_in = jnp.einsum("sf,df->sd", grad_projected, qkv_full, preferred_element_type=f32)
     grad_w_attn = jnp.concatenate([grad_w_qkv.astype(bf16), grad_w_out.astype(bf16)], axis=1)
     grad_attn_in, sum_attn = fused(
-        [share_sum(partial_attn_in.astype(bf16)), weight_sum(grad_w_attn)], "01011011", 7
+        [share_sum(partial_attn_in.astype(bf16)), weight_sum(grad_w_attn)], "1001111111", 7
     )
     grad_norm_in, grad_gain_one, grad_shift_one = norm_back(
         grad_attn_in, normed_one, inv_one, gain_one
@@ -862,11 +1114,11 @@
     out_down = sum_down.transpose(1, 0, 2).reshape(64, WIDTH)
 
     small = jnp.stack([grad_gain_one, grad_shift_one, grad_gain_two, grad_shift_two])
-    small = jnp.pad(small.reshape(4, 32, 64).transpose(1, 0, 2), ((0, 0), (0, 4), (0, 64)))
-    small = small_reduce(small, 10)[:4, :64]
-
     ends = jnp.stack([layer_out.astype(bf16), input_grad.astype(bf16)])
-    (tokens,) = fused([row_gather(ends)], "000", 8)
+    tokens, small = fused(
+        [row_gather(ends), small_reduce(jnp.pad(small, ((0, 4), (0, 0))))], "10101010", 8
+    )
+    small = jnp.where(odd, small[:4, 64:], small[:4, :64])
     tokens = tokens.reshape(2, 1, 512, WIDTH).astype(f32)
     return (
         tokens[0],

time: 510 us -> 470 us (0.922)
  the two profiles are of different devices: /device:TPU:1 before, /device:TPU:16 now
where the time goes in v3:
time: 470 us; the launch traced here: 463 us
  Pallas kernels  325 us (69%)
  matrix products  81.7 us (17%)
  local copies, waits for them, and re-layouts  36.9 us (8%)
  other arithmetic  18 us (4%)
    pallas_call x4, Pallas kernels, fused(): pl.pallas_call(functools.partial(fused_kernel, jobs, schedule), out_shape...  195 us
    pallas_call x2, Pallas kernels, kernel_call(): pl.pallas_call(kernel, out_shape=[shape for shape, _ in outs], in_specs=[...  130 us
    dot_general x1, matrix products, on_device(): grad_hidden = jnp.dot(cot, down_full, preferred_element_type=f32)  18.6 us
    dot_general x1, matrix products, on_device(): jnp.einsum('sd,sf->df', ffn_in, grad_up, preferred_element_type=f32)  9.45 us

profile of v3, /device:TPU:16, one launch (start us, length us, event | category | flops | bytes accessed | tf_op | source)
XLA Modules:
  0.0 462.6 jit_solution(782515453764910921)
XLA Ops:
  0.8 0.8 dynamic-slice_bitcast_fusion.1
  1.6 0.8 copy.63.refs_0_
  2.4 1.1 dynamic-slice_bitcast_fusion.refs_1_
  3.5 2.3 constant_dynamic-slice_fusion
  8.3 44.2 %shard_map.213 = (bf16[1,2,2,2,128,2048]{5,4,3,2,1,0:T(8,128)(2,1)}, bf16[1,2,2,2,128,2048]{5,4,3,2,1,0:T(8,128)(2,1)}, f32[128,2048]{1,0:T(8,128)}, f32[8,2048]...) custom-call(s32[256,1]{1,0:T(8,128)} %copy.63.refs_0_, ...), custom_call_target="tpu_custom_call" | custom-call | tf_op jit(solution)/shard_map/pallas_call | solution.py:128
  53.5 1.7 fusion.36
  55.1 0.8 bitcast_bitcast_fusion
  56.0 85.7 %shard_map.214 = (bf16[1024,768]{1,0:T(8,128)(2,1)}, bf16[1024,256]{1,0:T(8,128)(2,1)}, f32[128,2048]{1,0:T(8,128)}, bf16[2,2,2,128,2048]{4,3,2,1,0:T(8,128)(2,1...) custom-call(bf16[1024,2048]{1,0:T(8,128)(2,1)} %bitcast.151, bf16[2048,1024]{1,0:T(8,128)(2,1)} %bitcast.153, ...), custom_call_target="tpu_custom_call" | custom-call | tf_op jit(solution)/shard_map/pallas_call | solution.py:128
  141.7 18.6 %fusion.41 = f32[1024,1024]{1,0:T(8,128)S(1)} fusion(bf16[1024,2048]{1,0:T(8,128)(2,1)S(1)} %bitcast.191, bf16[2048,1024]{1,0:T(8,128)(2,1)} %bitcast.193), kind=kOutput, calls=%fused_computation.115 | convolution fusion | flops 4294967296 | bytes 12582912 | tf_op jit(solution)/shard_map/dot_general | solution.py:1052
  160.3 6.7 %fusion.7 = (bf16[1024,1024]{1,0:T(8,128)(2,1)S(1)}, f32[1024,1024]{1,0:T(8,128)S(1)}) fusion(f32[1024,1024]{1,0:T(8,128)S(1)} %fusion.41, bf16[1024,2048]{1,0:T(8,128)(2,1)S(1)} %bitcast.190, bf16[2048,1024]{1,0:T(8,128)(2,1)S(1)} %bitcast.195), kind=kOutput, calls=%fused_computation.9 | convolution fusion | flops 4315938816 | bytes 18874368 | tf_op jit(solution)/shard_map/dot_general | solution.py:1048
  167.1 6.2 %convolution_convert_fusion.4 = bf16[1024,2048]{1,0:T(8,128)(2,1)} fusion(bf16[1024,1024]{1,0:T(8,128)(2,1)S(1)} %get-tuple-element.78, bf16[2048,1024]{1,0:T(8,128)(2,1)S(1)} %bitcast.196), kind=kOutput, calls=%fused_computation.20 | convolution fusion | flops 4297064448 | bytes 10485760 | tf_op jit(solution)/shard_map/sf,df->sd/dot_general | solution.py:1056
  173.3 6.6 %convolution_convert_fusion.3 = bf16[1024,2048]{1,0:T(8,128)(2,1)} fusion(bf16[2048,1024]{1,0:T(8,128)(2,1)S(1)} %bitcast.194, f32[1024,1024]{1,0:T(8,128)S(1)} %get-tuple-element.79), kind=kOutput, calls=%fused_computation.19 | convolution fusion | flops 4306501632 | bytes 12582912 | tf_op jit(solution)/shard_map/sf,df->sd/dot_general | solution.py:1050
  179.9 6.4 %convolution_convert_fusion.2 = bf16[2048,1024]{1,0:T(8,128)(2,1)} fusion(bf16[1024,2048]{1,0:T(8,128)(2,1)S(1)} %bitcast.192, f32[1024,1024]{1,0:T(8,128)S(1)} %get-tuple-element.79), kind=kOutput, calls=%fused_computation.18 | convolution fusion | flops 4306501632 | bytes 12582912 | tf_op jit(solution)/shard_map/sd,sf->df/dot_general | solution.py:1051
  186.3 75.2 %shard_map.215 = (f32[128,2048]{1,0:T(8,128)}, f32[128,2048]{1,0:T(8,128)}, bf16[2,64,1024]{2,1,0:T(8,128)(2,1)}) custom-call(bf16[2,2,2,128,2048]{4,3,2,1,0:T(8,128)(2,1)} %bitcast.146, bf16[2,2,2,128,2048]{4,3,2,1,0:T(8,128)(2,1)} %bitcast.147, bf16[2,4,4,64,1024]{4,3,2,1,0:T(8,128)(2,1)} %bitcast.148), custom_call_target="tpu_custom_call" | custom-call | tf_op jit(solution)/shard_map/pallas_call | solution.py:170
  261.9 0.9 fusion.39
  262.9 2.7 multiply_reduce_fusion.1
  265.7 2.8 fusion.35
  269.1 0.9 copy.66
  270.1 0.8 copy.74
  270.9 3.8 fusion.40
  274.7 9.5 %convolution_convert_fusion.1 = bf16[2048,1024]{1,0:T(8,128)(2,1)} fusion(bf16[1024,2048]{1,0:T(8,128)(2,1)} %bitcast.189, bf16[1024,1024]{1,0:T(8,128)(2,1)} %copy-done.29), kind=kOutput, calls=%fused_computation.17 | convolution fusion | flops 4297064448 | bytes 10485760 | tf_op jit(solution)/shard_map/sd,sf->df/dot_general | solution.py:1055
  284.2 39.8 %shard_map.216 = (bf16[2,2,2,128,2048]{4,3,2,1,0:T(8,128)(2,1)S(1)}, bf16[2,64,1024]{2,1,0:T(8,128)(2,1)S(1)}) custom-call(bf16[128,2048]{1,0:T(8,128)(2,1)S(1)} %get-tuple-element.60.refs_0_, bf16[2,4,4,64,1024]{4,3,2,1,0:T(8,128)(2,1)} %bitcast.150), custom_call_target="tpu_custom_call" | custom-call | tf_op jit(solution)/shard_map/pallas_call | solution.py:170
  324.0 2.0 copy-done.3
  326.0 2.5 convolution_convert_fusion.7
  329.2 3.0 multiply_reduce_fusion
  332.7 1.2 multiply_convert_fusion
  333.9 1.3 fusion.21
  335.1 1.3 copy.73
  336.4 0.9 bitcast_dynamic-update-slice_fusion.2
  337.4 0.8 fusion.20
  338.8 1.0 bitcast_dynamic-update-slice_fusion.1
  339.7 3.2 fusion.22
  343.3 0.9 bitcast_dynamic-update-slice_fusion
  344.3 8.0 %convolution_convert_fusion = bf16[1024,2048]{1,0:T(8,128)(2,1)} fusion(bf16[1024,768]{1,0:T(8,128)(2,1)} %bitcast_dynamic-update-slice_fusion, bf16[2048,1024]{1,0:T(8,128)(2,1)} %bitcast.155), kind=kOutput, calls=%fused_computation.16 | convolution fusion | flops 3223322624 | bytes 8912896 | tf_op jit(solution)/shard_map/sf,df->sd/dot_general | solution.py:1100
  352.3 1.3 convolution_convert_fusion.6
  353.6 0.9 copy-done.8
  354.9 3.8 convolution_convert_fusion.5
  358.8 2.4 pad_maximum_fusion
  361.2 6.4 %copy.80 = bf16[2048,1024]{1,0:T(8,128)(2,1)} copy(bf16[2048,1024]{0,1:T(8,128)(2,1)} %pad_maximum_fusion) | data formatting | bytes 8388608 | tf_op jit(solution)/shard_map/concatenate | solution.py:1101
  367.6 2.2 copy-done.2
  369.8 47.7 %shard_map.217 = (f32[128,2048]{1,0:T(8,128)S(1)}, bf16[2,64,1024]{2,1,0:T(8,128)(2,1)S(1)}) custom-call(bf16[2,2,2,128,2048]{4,3,2,1,0:T(8,128)(2,1)S(1)} %bitcast.142, bf16[2,4,4,64,1024]{4,3,2,1,0:T(8,128)(2,1)} %bitcast.145), custom_call_target="tpu_custom_call" | custom-call | tf_op jit(solution)/shard_map/pallas_call | solution.py:170
  418.4 1.7 fusion.27
  420.3 32.0 %shard_map.218 = (bf16[2,2,2,128,2048]{4,3,2,1,0:T(8,128)(2,1)S(1)}, f32[8,128]{1,0:T(8,128)S(1)}) custom-call(bf16[2,128,2048]{2,1,0:T(8,128)(2,1)S(1)} %pad_maximum_fusion.1.refs_0_, f32[8,2048]{1,0:T(8,128)S(1)} %select_maximum_fusion.refs_1_), custom_call_target="tpu_custom_call" | custom-call | tf_op jit(solution)/shard_map/pallas_call | solution.py:170
  452.3 4.5 fusion.37
  457.9 1.1 reshape.296
  459.8 0.8 copy.92
  460.6 1.0 convert_bitcast_fusion
  461.6 0.8 copy.93
  (105 shorter events, 10.2 us)
Async XLA Ops:
  0.6 1.7 copy-start
  0.7 5.1 %copy-start.17 = (bf16[64,512]{1,0:T(8,128)(2,1)S(1)}, bf16[64,512]{1,0:T(8,128)(2,1)}, u32[]{:S(2)}) copy-start(bf16[64,512]{1,0:T(8,128)(2,1)} %param.22) | copy-start | bytes 196612
  0.7 5.1 %copy-start.15 = (bf16[64,3,512]{2,0,1:T(8,128)(2,1)S(1)}, bf16[64,3,512]{2,0,1:T(8,128)(2,1)}, u32[]{:S(2)}) copy-start(bf16[64,3,512]{2,0,1:T(8,128)(2,1)} %param.21) | copy-start | bytes 589828
  0.7 6.3 %copy-start.20 = (bf16[64]{0:T(256)(128)(2,1)S(1)}, bf16[64]{0:T(256)(128)(2,1)}, u32[]{:S(2)}) copy-start(bf16[64]{0:T(256)(128)(2,1)} %param.24) | copy-start | bytes 388
  0.7 6.3 %copy-start.21 = (bf16[64]{0:T(256)(128)(2,1)S(1)}, bf16[64]{0:T(256)(128)(2,1)}, u32[]{:S(2)}) copy-start(bf16[64]{0:T(256)(128)(2,1)} %param.23) | copy-start | bytes 388
  0.7 6.3 %copy-start.22 = (bf16[64]{0:T(256)(128)(2,1)S(1)}, bf16[64]{0:T(256)(128)(2,1)}, u32[]{:S(2)}) copy-start(bf16[64]{0:T(256)(128)(2,1)} %param.20) | copy-start | bytes 388
  0.7 6.3 %copy-start.23 = (bf16[64]{0:T(256)(128)(2,1)S(1)}, bf16[64]{0:T(256)(128)(2,1)}, u32[]{:S(2)}) copy-start(bf16[64]{0:T(256)(128)(2,1)} %param.19) | copy-start | bytes 388
  0.7 7.0 %copy-start.18 = (s32[1,512]{1,0:T(1,128)S(1)}, s32[1,512]{1,0:T(1,128)}, u32[]{:S(2)}) copy-start(s32[1,512]{1,0:T(1,128)} %param.17) | copy-start | bytes 6148
  0.7 7.0 %copy-start.19 = (s32[1,512]{1,0:T(1,128)S(1)}, s32[1,512]{1,0:T(1,128)}, u32[]{:S(2)}) copy-start(s32[1,512]{1,0:T(1,128)} %param.16) | copy-start | bytes 6148
  8.3 46.9 %copy-start.13 = (bf16[64,2048]{1,0:T(8,128)(2,1)S(1)}, bf16[64,2048]{1,0:T(8,128)(2,1)}, u32[]{:S(2)}) copy-start(bf16[64,2048]{1,0:T(8,128)(2,1)} %param.26) | copy-start | bytes 786436
  8.3 46.9 %copy-start.14 = (bf16[64,2048]{1,0:T(8,128)(2,1)S(1)}, bf16[64,2048]{1,0:T(8,128)(2,1)}, u32[]{:S(2)}) copy-start(bf16[64,2048]{1,0:T(8,128)(2,1)} %param.25) | copy-start | bytes 786436
  56.0 85.7 %copy-start.25 = (bf16[1,2,2,2,128,2048]{5,4,3,2,1,0:T(8,128)(2,1)S(1)}, bf16[1,2,2,2,128,2048]{5,4,3,2,1,0:T(8,128)(2,1)}, u32[]{:S(2)}) copy-start(bf16[1,2,2,2,128,2048]{5,4,3,2,1,0:T(8,128)(2,1)} %get-tuple-element.37) | copy-start | bytes 12582916
  141.7 18.6 %copy-start.24 = (bf16[2,2,2,128,2048]{4,3,2,1,0:T(8,128)(2,1)S(1)}, bf16[2,2,2,128,2048]{4,3,2,1,0:T(8,128)(2,1)}, u32[]{:S(2)}) copy-start(bf16[2,2,2,128,2048]{4,3,2,1,0:T(8,128)(2,1)} %get-tuple-element.39) | copy-start | bytes 12582916
  141.7 18.6 %copy-start.27 = (bf16[2,4,4,64,1024]{4,3,2,1,0:T(8,128)(2,1)S(1)}, bf16[2,4,4,64,1024]{4,3,2,1,0:T(8,128)(2,1)}, u32[]{:S(2)}) copy-start(bf16[2,4,4,64,1024]{4,3,2,1,0:T(8,128)(2,1)} %get-tuple-element.40) | copy-start | bytes 12582916
  167.1 6.2 %copy-start.29 = (bf16[1024,1024]{1,0:T(8,128)(2,1)}, bf16[1024,1024]{1,0:T(8,128)(2,1)S(1)}, u32[]{:S(2)}) copy-start(bf16[1024,1024]{1,0:T(8,128)(2,1)S(1)} %get-tuple-element.78) | copy-start | bytes 6291460
  167.1 6.2 %copy-start.26 = (bf16[2,4,4,64,1024]{4,3,2,1,0:T(8,128)(2,1)S(1)}, bf16[2,4,4,64,1024]{4,3,2,1,0:T(8,128)(2,1)}, u32[]{:S(2)}) copy-start(bf16[2,4,4,64,1024]{4,3,2,1,0:T(8,128)(2,1)} %get-tuple-element.38) | copy-start | bytes 12582916
  186.3 75.2 %copy-start.6 = (f32[128,2048]{1,0:T(8,128)S(1)}, f32[128,2048]{1,0:T(8,128)}, u32[]{:S(2)}) copy-start(f32[128,2048]{1,0:T(8,128)} %get-tuple-element.36) | copy-start | bytes 3145732
  261.5 4.1 copy-start.9
  265.6 2.8 copy-start.11
  324.0 2.0 copy-start.3
  329.0 3.2 copy-start.12
  329.2 3.5 copy-start.7
  344.3 8.0 %copy-start.4 = (bf16[2,2,2,128,2048]{4,3,2,1,0:T(8,128)(2,1)S(1)}, bf16[2,2,2,128,2048]{4,3,2,1,0:T(8,128)(2,1)}, u32[]{:S(2)}) copy-start(bf16[2,2,2,128,2048]{4,3,2,1,0:T(8,128)(2,1)} %copy-done.3) | copy-start | bytes 12582916
  344.3 8.0 %copy-start.28 = (bf16[1024,256]{1,0:T(8,128)(2,1)S(1)}, bf16[1024,256]{1,0:T(8,128)(2,1)}, u32[]{:S(2)}) copy-start(bf16[1024,256]{1,0:T(8,128)(2,1)} %get-tuple-element.45) | copy-start | bytes 1572868
  352.3 2.2 copy-start.8
  352.3 2.7 copy-start.16
  367.6 2.2 copy-start.2
  369.8 47.7 %copy-start.5 = (f32[128,2048]{1,0:T(8,128)S(1)}, f32[128,2048]{1,0:T(8,128)}, u32[]{:S(2)}) copy-start(f32[128,2048]{1,0:T(8,128)} %get-tuple-element.34.refs_3_) | copy-start | bytes 3145732
  417.5 2.6 copy-start.10
  457.4 5.1 %copy-start.1 = (bf16[1,512,2048]{2,1,0:T(8,128)(2,1)S(1)}, bf16[1,512,2048]{2,1,0:T(8,128)(2,1)}, u32[]{:S(2)}) copy-start(bf16[1,512,2048]{2,1,0:T(8,128)(2,1)} %param.14) | copy-start | bytes 6291460
